TPU v7x, 256 devices: a whole 4x4x8 slice. The times are simulated.
256 devices in a mesh: tm: 8 (over x, core), space: 32 (over y, z).
Axes of the slice: x: 4, y: 4, z: 8, core: 2. Of those that a mesh axis runs over, the one named last changes fastest.
Arguments:
- queries: bfloat16 [32768, 4096], P(('tm', 'space')), may hold values from -4.5 to 4.5
- key_rows: bfloat16 [32768, 4096], P(('tm', 'space')), may hold values from -4.5 to 4.5
- value_rows: bfloat16 [32768, 4096], P(('tm', 'space')), may hold values from -6 to 6
- grads_out: bfloat16 [32768, 4096], P(('tm', 'space')), may hold values from -12 to 12
- block_lists: int32 [8, 32, 13], P('tm'), may hold values from 0 to 255, as said below
- block_counts: int32 [8, 32], P('tm'), may hold values from 1 to 13
Outputs:
- grad_queries: bfloat16 [32768, 4096], P(('tm', 'space'))
- grad_keys: bfloat16 [32768, 4096], P(('tm', 'space'))
- grad_values: bfloat16 [32768, 4096], P(('tm', 'space'))
Inputs may be any that keep to these rules, and one draw needn't show every extreme that they name: For c < block_counts[f, i], block_lists[f, i, c] names distinct blocks g * 32 + j with |g - f| <= 2 and |j - i| <= 2 - |g - f|; every list names the block f * 32 + i; slots from block_counts[f, i] on hold f * 32 + i.
All inputs are finite; a program needn't handle non-finite values.
Results may differ from a plain program's by a relative error of at most 0.022.
Values may be sent and summed in bfloat16 or wider, within the bound.
A program may use at most 192 MiB of HBM per device.

v0:
```python
import jax
import jax.numpy as jnp
from jax import lax
from jax.sharding import PartitionSpec as P

HD = 128
BLK = 128


def from_behind(block, axis, distance):
    devices = range(lax.axis_size(axis))
    route = [(i - distance, i) for i in devices if i - distance in devices]
    return lax.ppermute(block, axis, route)


def fast_product(pattern, first_op, second_op):
    return jnp.einsum(pattern, first_op, second_op, preferred_element_type=jnp.float32)


def band_grads(
    queries, grads_out, key_rows, value_rows, block_ids, counts, block_len, head_dim, product
):
    frame_len, width = queries.shape
    head_count = width // head_dim
    query_blocks = frame_len // block_len
    key_blocks = key_rows.shape[0] // block_len
    listed = block_ids.shape[1]
    group_size = min(query_blocks, max(1, 512 // block_len))
    group_steps = query_blocks // group_size
    score_scale = head_dim ** (-0.5)
    query_groups = queries.reshape(group_steps, group_size, block_len, head_count, head_dim)
    grad_groups = grads_out.reshape(group_steps, group_size, block_len, head_count, head_dim)
    key_tiles = key_rows.reshape(key_blocks, block_len, head_count, head_dim)
    value_tiles = value_rows.reshape(key_blocks, block_len, head_count, head_dim)
    id_groups = block_ids.reshape(group_steps, group_size, listed)
    count_groups = counts.reshape(group_steps, group_size)
    slot_index = jnp.arange(listed, dtype=jnp.int32)

    def one_group(totals, inputs):
        query_group, grad_group, id_group, count_group = inputs
        gathered_keys = key_tiles[id_group].reshape(
            group_size, listed * block_len, head_count, head_dim
        )
        gathered_values = value_tiles[id_group].reshape(
            group_size, listed * block_len, head_count, head_dim
        )
        live_mask = slot_index[None, :] < count_group[:, None]
        live_mask = jnp.broadcast_to(live_mask[:, :, None], (group_size, listed, block_len))
        live_mask = live_mask.reshape(group_size, 1, 1, listed * block_len)
        scores = product("gqhd,gkhd->ghqk", query_group, gathered_keys) * score_scale
        scores = jnp.where(live_mask, scores, -1e30)
        row_top = jnp.max(scores, axis=-1, keepdims=True)
        row_total = jnp.sum(jnp.exp(scores - row_top), axis=-1, keepdims=True)
        log_total = row_top + jnp.log(row_total)
        probs = jnp.exp(scores - log_total)
        probs_low = probs.astype(jnp.bfloat16)
        attention_out = product("ghqk,gkhd->gqhd", probs_low, gathered_values).astype(jnp.bfloat16)
        deltas = jnp.sum(
            grad_group.astype(jnp.float32) * attention_out.astype(jnp.float32), axis=-1
        )
        grad_probs = product("gqhd,gkhd->ghqk", grad_group, gathered_values)
        grad_scores = (probs * (grad_probs - jnp.transpose(deltas, (0, 2, 1))[..., None])).astype(
            jnp.bfloat16
        )
        grad_query = product("ghqk,gkhd->gqhd", grad_scores, gathered_keys) * score_scale
        grad_key = product("ghqk,gqhd->gkhd", grad_scores, query_group) * score_scale
        grad_value = product("ghqk,gqhd->gkhd", probs_low, grad_group)
        update = jnp.stack([grad_key, grad_value]).reshape(2, group_size * listed, block_len, width)
        totals = totals.at[:, id_group.reshape(-1)].add(update)
        return (totals, grad_query.reshape(group_size * block_len, width))

    start_totals = jnp.zeros((2, key_blocks, block_len, width), jnp.float32)
    totals, grad_rows = lax.scan(
        one_group, start_totals, (query_groups, grad_groups, id_groups, count_groups)
    )
    return (grad_rows.reshape(frame_len, width), totals.reshape(2, key_blocks * block_len, width))


def local(queries, key_rows, value_rows, grads_out, block_lists, block_counts):
    query_here, key_here, value_here, grad_here = (
        lax.all_to_all(queries, "space", split_axis=1, concat_axis=0, tiled=True),
        lax.all_to_all(key_rows, "space", split_axis=1, concat_axis=0, tiled=True),
        lax.all_to_all(value_rows, "space", split_axis=1, concat_axis=0, tiled=True),
        lax.all_to_all(grads_out, "space", split_axis=1, concat_axis=0, tiled=True),
    )
    frame_len = query_here.shape[0]
    query_blocks = frame_len // BLK
    frame_here = lax.axis_index("tm")
    key_value = jnp.stack([key_here, value_here])
    pieces = []
    for offset in (-2, -1, 0, 1, 2):
        if offset == 0:
            pieces.append(key_value)
        else:
            pieces.append(from_behind(key_value, "tm", -offset))
    every_frame = jnp.concatenate(pieces, axis=1)
    local_ids = block_lists[0] - (frame_here - 2) * query_blocks
    grad_query, partial_value = band_grads(
        query_here,
        grad_here,
        every_frame[0],
        every_frame[1],
        local_ids,
        block_counts[0],
        BLK,
        HD,
        fast_product,
    )
    grad_query = grad_query.astype(jnp.bfloat16)
    rounded = partial_value.astype(jnp.bfloat16)
    summed = rounded[:, 2 * frame_len : 3 * frame_len].astype(jnp.float32)
    for offset in (-2, -1, 1, 2):
        start_row = (offset + 2) * frame_len
        arrived = from_behind(rounded[:, start_row : start_row + frame_len], "tm", offset)
        summed = summed + arrived.astype(jnp.float32)
    key_grad = summed[0].astype(jnp.bfloat16)
    value_grad = summed[1].astype(jnp.bfloat16)
    query_final, key_final, value_final = (
        lax.all_to_all(grad_query, "space", split_axis=0, concat_axis=1, tiled=True),
        lax.all_to_all(key_grad, "space", split_axis=0, concat_axis=1, tiled=True),
        lax.all_to_all(value_grad, "space", split_axis=0, concat_axis=1, tiled=True),
    )
    return (query_final, key_final, value_final)


def solution(mesh):
    placed = (
        P(("tm", "space"), None),
        P(("tm", "space"), None),
        P(("tm", "space"), None),
        P(("tm", "space"), None),
        P("tm", None, None),
        P("tm", None),
    )
    return jax.shard_map(
        local,
        mesh=mesh,
        in_specs=placed,
        out_specs=(P(("tm", "space"), None), P(("tm", "space"), None), P(("tm", "space"), None)),
        check_vma=False,
    )
```

profile of v0, /device:TPU:2, one launch (start us, length us, event | category | flops | bytes accessed | tf_op | source)
XLA Modules:
  0.0 821.5 jit_solution(12363593859155738468)
XLA Ops:
  3.1 11.5 %all-to-all-start.1 = ((bf16[128,32,128]{2,0,1:T(8,128)(2,1)}), bf16[128,32,128]{2,0,1:T(8,128)(2,1)S(1)}, u32[]{:S(2)}, u32[]{:S(2)}) async-start(bf16[128,32,128]{2,0,1:T(8,128)(2,1)} %copy_bitcast_fusion.2), calls=%async_computation.1 | async-start | bytes 2097152 | tf_op jit(solution)/shard_map/all_to_all | solution.py:82
  14.9 28.3 %all-to-all-done.1 = bf16[128,32,128]{2,0,1:T(8,128)(2,1)S(1)} async-done(((bf16[128,32,128]{2,0,1:T(8,128)(2,1)}), bf16[128,32,128]{2,0,1:T(8,128)(2,1)S(1)}, u32[]{:S(2)}, u32[]{:S(2)}) %all-to-all-start.1) | async-done | bytes 1048608 | tf_op jit(solution)/shard_map/all_to_all | solution.py:82
  43.3 33.3 %all_to_all.112 = bf16[128,32,128]{2,0,1:T(8,128)(2,1)S(1)} all-to-all(bf16[128,32,128]{2,0,1:T(8,128)(2,1)S(1)} %copy_bitcast_fusion.1), channel_id=1, replica_groups=mesh['tm'=8,'space'=32] {'space'}, dimensions={1} | all-to-all | bytes 2097152 | tf_op jit(solution)/shard_map/all_to_all | solution.py:83
  99.0 29.9 %collective-permute-done = bf16[2,4096,128]{2,1,0:T(8,128)(2,1)} collective-permute-done((bf16[2,4096,128]{2,1,0:T(8,128)(2,1)}, bf16[2,4096,128]{2,1,0:T(8,128)(2,1)}, u32[]{:S(2)}, u32[]{:S(2)}) %collective-permute-start) | collective-permute-done | bytes 2097184 | tf_op jit(solution)/shard_map/ppermute | solution.py:13
  132.1 13.7 %collective-permute-done.1 = bf16[2,4096,128]{2,1,0:T(8,128)(2,1)} collective-permute-done((bf16[2,4096,128]{2,1,0:T(8,128)(2,1)}, bf16[2,4096,128]{2,1,0:T(8,128)(2,1)}, u32[]{:S(2)}, u32[]{:S(2)}) %collective-permute-start.1) | collective-permute-done | bytes 2097184 | tf_op jit(solution)/shard_map/ppermute | solution.py:13
  160.8 5.5 all-to-all-start.3
  166.3 9.0 %fusion.26 = (bf16[1,20480,128]{2,1,0:T(8,128)(2,1)}, bf16[1,20480,128]{2,1,0:T(8,128)(2,1)}) fusion(bf16[2,20480,128]{2,1,0:T(8,128)(2,1)} %constant_dynamic-update-slice_fusion.1), kind=kLoop, calls=%fused_computation.56 | loop fusion | bytes 20971520 | tf_op jit(solution)/shard_map/slice | solution.py:102
  175.3 18.9 %all-to-all-done.3 = bf16[128,32,128]{0,2,1:T(8,128)(2,1)S(1)} async-done(((bf16[128,32,128]{0,2,1:T(8,128)(2,1)}), bf16[128,32,128]{0,2,1:T(8,128)(2,1)S(1)}, u32[]{:S(2)}, u32[]{:S(2)}) %all-to-all-start.3) | async-done | bytes 1048608 | tf_op jit(solution)/shard_map/all_to_all | solution.py:84
  194.2 9.7 %broadcast_in_dim.37 = f32[2,160,128,128]{3,2,1,0:T(8,128)} broadcast(f32[]{:T(128)} %constant.10.clone.1), dimensions={} | broadcast | bytes 20971524 | tf_op jit(solution)/shard_map/broadcast_in_dim | solution.py:72
  203.9 454.9 %while.13 = (s32[]{:T(128)}, f32[2,160,128,128]{3,2,1,0:T(8,128)}, bf16[8,512,128]{2,1,0:T(8,128)(2,1)}, s32[8,4,13]{2,1,0:T(4,128)S(1)}, bf16[8,4,128,1,128]{4,...) while((s32[]{:T(128)}, f32[2,160,128,128]{3,2,1,0:T(8,128)}, ...), condition=%wide.region_5.6_spmd.clone, body=%wide.region_0.5_spmd.clone.sunk | while | flops 1324417408 | bytes 142269568 | solution.py:73
  242.0 18.3 %scatter_fusion = f32[2,160,128,128]{3,2,1,0:T(8,128)} fusion(f32[2,160,128,128]{3,2,1,0:T(8,128)} %get-tuple-element.191, s32[52]{0:T(128)S(1)} %fusion.63, f32[52,2,128,128]{3,2,1,0:T(8,128)} %copy.104), kind=kCustom, calls=%fused_computation.2.clone.clone.1 | custom fusion | flops 1703936 | bytes 20447440 | tf_op jit(solution)/shard_map/while/body/eval_jaxpr/scatter-add | solution.py:69
  298.4 19.1 %scatter_fusion = f32[2,160,128,128]{3,2,1,0:T(8,128)} fusion(f32[2,160,128,128]{3,2,1,0:T(8,128)} %get-tuple-element.191, s32[52]{0:T(128)S(1)} %fusion.63, f32[52,2,128,128]{3,2,1,0:T(8,128)} %copy.104), kind=kCustom, calls=%fused_computation.2.clone.clone.1 | custom fusion | flops 1703936 | bytes 20447440 | tf_op jit(solution)/shard_map/while/body/eval_jaxpr/scatter-add | solution.py:69
  355.6 18.8 %scatter_fusion = f32[2,160,128,128]{3,2,1,0:T(8,128)} fusion(f32[2,160,128,128]{3,2,1,0:T(8,128)} %get-tuple-element.191, s32[52]{0:T(128)S(1)} %fusion.63, f32[52,2,128,128]{3,2,1,0:T(8,128)} %copy.104), kind=kCustom, calls=%fused_computation.2.clone.clone.1 | custom fusion | flops 1703936 | bytes 20447440 | tf_op jit(solution)/shard_map/while/body/eval_jaxpr/scatter-add | solution.py:69
  412.6 18.6 %scatter_fusion = f32[2,160,128,128]{3,2,1,0:T(8,128)} fusion(f32[2,160,128,128]{3,2,1,0:T(8,128)} %get-tuple-element.191, s32[52]{0:T(128)S(1)} %fusion.63, f32[52,2,128,128]{3,2,1,0:T(8,128)} %copy.104), kind=kCustom, calls=%fused_computation.2.clone.clone.1 | custom fusion | flops 1703936 | bytes 20447440 | tf_op jit(solution)/shard_map/while/body/eval_jaxpr/scatter-add | solution.py:69
  469.3 18.8 %scatter_fusion = f32[2,160,128,128]{3,2,1,0:T(8,128)} fusion(f32[2,160,128,128]{3,2,1,0:T(8,128)} %get-tuple-element.191, s32[52]{0:T(128)S(1)} %fusion.63, f32[52,2,128,128]{3,2,1,0:T(8,128)} %copy.104), kind=kCustom, calls=%fused_computation.2.clone.clone.1 | custom fusion | flops 1703936 | bytes 20447440 | tf_op jit(solution)/shard_map/while/body/eval_jaxpr/scatter-add | solution.py:69
  526.3 18.4 %scatter_fusion = f32[2,160,128,128]{3,2,1,0:T(8,128)} fusion(f32[2,160,128,128]{3,2,1,0:T(8,128)} %get-tuple-element.191, s32[52]{0:T(128)S(1)} %fusion.63, f32[52,2,128,128]{3,2,1,0:T(8,128)} %copy.104), kind=kCustom, calls=%fused_computation.2.clone.clone.1 | custom fusion | flops 1703936 | bytes 20447440 | tf_op jit(solution)/shard_map/while/body/eval_jaxpr/scatter-add | solution.py:69
  582.8 18.7 %scatter_fusion = f32[2,160,128,128]{3,2,1,0:T(8,128)} fusion(f32[2,160,128,128]{3,2,1,0:T(8,128)} %get-tuple-element.191, s32[52]{0:T(128)S(1)} %fusion.63, f32[52,2,128,128]{3,2,1,0:T(8,128)} %copy.104), kind=kCustom, calls=%fused_computation.2.clone.clone.1 | custom fusion | flops 1703936 | bytes 20447440 | tf_op jit(solution)/shard_map/while/body/eval_jaxpr/scatter-add | solution.py:69
  639.6 19.2 %scatter_fusion = f32[2,160,128,128]{3,2,1,0:T(8,128)} fusion(f32[2,160,128,128]{3,2,1,0:T(8,128)} %get-tuple-element.191, s32[52]{0:T(128)S(1)} %fusion.63, f32[52,2,128,128]{3,2,1,0:T(8,128)} %copy.104), kind=kCustom, calls=%fused_computation.2.clone.clone.1 | custom fusion | flops 1703936 | bytes 20447440 | tf_op jit(solution)/shard_map/while/body/eval_jaxpr/scatter-add | solution.py:69
  658.7 8.2 convert_element_type.76
  690.0 28.8 %collective-permute-done.4 = bf16[2,4096,128]{2,1,0:T(8,128)(2,1)S(1)} collective-permute-done((bf16[2,4096,128]{2,1,0:T(8,128)(2,1)}, bf16[2,4096,128]{2,1,0:T(8,128)(2,1)S(1)}, u32[]{:S(2)}, u32[]{:S(2)}) %collective-permute-start.4) | collective-permute-done | bytes 2097184 | tf_op jit(solution)/shard_map/ppermute | solution.py:13
  718.8 7.3 collective-permute-done.7
  726.2 17.2 %collective-permute-done.6 = bf16[2,4096,128]{2,1,0:T(8,128)(2,1)} collective-permute-done((bf16[2,4096,128]{2,1,0:T(8,128)(2,1)}, bf16[2,4096,128]{2,1,0:T(8,128)(2,1)}, u32[]{:S(2)}, u32[]{:S(2)}) %collective-permute-start.6) | collective-permute-done | bytes 2097184 | tf_op jit(solution)/shard_map/ppermute | solution.py:13
  749.3 37.0 %all_to_all.113 = bf16[32,128,128]{2,1,0:T(8,128)(2,1)S(1)} all-to-all(bf16[32,128,128]{2,1,0:T(8,128)(2,1)S(1)} %bitcast.197), channel_id=1, replica_groups=mesh['tm'=8,'space'=32] {'space'}, dimensions={0} | all-to-all | bytes 2097152 | tf_op jit(solution)/shard_map/all_to_all | solution.py:120
  798.4 21.2 %all-to-all-done.6 = bf16[32,128,128]{2,1,0:T(8,128)(2,1)S(1)} async-done(((bf16[32,128,128]{2,1,0:T(8,128)(2,1)}), bf16[32,128,128]{2,1,0:T(8,128)(2,1)S(1)}, u32[]{:S(2)}, u32[]{:S(2)}) %all-to-all-start.6) | async-done | bytes 1048608 | tf_op jit(solution)/shard_map/all_to_all | solution.py:121
  (359 shorter events, 390.6 us)
Async XLA Ops:
  3.1 40.1 %all-to-all-start.1 = ((bf16[128,32,128]{2,0,1:T(8,128)(2,1)}), bf16[128,32,128]{2,0,1:T(8,128)(2,1)S(1)}, u32[]{:S(2)}, u32[]{:S(2)}) async-start(bf16[128,32,128]{2,0,1:T(8,128)(2,1)} %copy_bitcast_fusion.2), calls=%async_computation.1 | async-start | bytes 2097152 | tf_op jit(solution)/shard_map/all_to_all | solution.py:82
  43.3 43.8 %copy-start.11 = (bf16[128,4096]{1,0:T(8,128)(2,1)S(1)}, bf16[128,4096]{1,0:T(8,128)(2,1)}, u32[]{:S(2)}) copy-start(bf16[128,4096]{1,0:T(8,128)(2,1)} %param.8) | copy-start | bytes 3145732
  76.6 19.3 %copy-start.13 = (s32[1,32]{1,0:T(1,128)S(1)}, s32[1,32]{1,0:T(1,128)}, u32[]{:S(2)}) copy-start(s32[1,32]{1,0:T(1,128)} %param.13) | copy-start | bytes 388
  78.1 50.8 %collective-permute-start = (bf16[2,4096,128]{2,1,0:T(8,128)(2,1)}, bf16[2,4096,128]{2,1,0:T(8,128)(2,1)}, u32[]{:S(2)}, u32[]{:S(2)}) collective-permute-start(bf16[2,4096,128]{2,1,0:T(8,128)(2,1)} %pad_maximum_fusion), channel_id=1, source_target_pairs={{0,64},{32,96},{64,128},{96,160},{128,192},{160,224},{1,65},{33,97... | collective-permute-start | bytes 6291464 | tf_op jit(solution)/shard_map/ppermute | solution.py:13
  81.5 64.3 %collective-permute-start.1 = (bf16[2,4096,128]{2,1,0:T(8,128)(2,1)}, bf16[2,4096,128]{2,1,0:T(8,128)(2,1)}, u32[]{:S(2)}, u32[]{:S(2)}) collective-permute-start(bf16[2,4096,128]{2,1,0:T(8,128)(2,1)} %pad_maximum_fusion), channel_id=1, source_target_pairs={{0,32},{32,64},{64,96},{96,128},{128,160},{160,192},{192,224},{1,3... | collective-permute-start | bytes 6291464 | tf_op jit(solution)/shard_map/ppermute | solution.py:13
  83.4 67.3 %collective-permute-start.2 = (bf16[2,4096,128]{2,1,0:T(8,128)(2,1)}, bf16[2,4096,128]{2,1,0:T(8,128)(2,1)}, u32[]{:S(2)}, u32[]{:S(2)}) collective-permute-start(bf16[2,4096,128]{2,1,0:T(8,128)(2,1)} %pad_maximum_fusion), channel_id=1, source_target_pairs={{32,0},{64,32},{96,64},{128,96},{160,128},{192,160},{224,192},{33,... | collective-permute-start | bytes 6291464 | tf_op jit(solution)/shard_map/ppermute | solution.py:13
  88.3 72.5 %all-to-all-start = ((bf16[128,32,128]{2,0,1:T(8,128)(2,1)}), bf16[128,32,128]{2,0,1:T(8,128)(2,1)S(1)}, u32[]{:S(2)}, u32[]{:S(2)}) async-start(bf16[128,32,128]{2,0,1:T(8,128)(2,1)} %copy_bitcast_fusion.3), calls=%async_computation | async-start | bytes 2097152 | tf_op jit(solution)/shard_map/all_to_all | solution.py:81
  93.3 64.3 %collective-permute-start.3 = (bf16[2,4096,128]{2,1,0:T(8,128)(2,1)}, bf16[2,4096,128]{2,1,0:T(8,128)(2,1)}, u32[]{:S(2)}, u32[]{:S(2)}) collective-permute-start(bf16[2,4096,128]{2,1,0:T(8,128)(2,1)} %pad_maximum_fusion), channel_id=1, source_target_pairs={{64,0},{96,32},{128,64},{160,96},{192,128},{224,160},{65,1},{97,33... | collective-permute-start | bytes 6291464 | tf_op jit(solution)/shard_map/ppermute | solution.py:13
  160.8 33.4 %all-to-all-start.3 = ((bf16[128,32,128]{0,2,1:T(8,128)(2,1)}), bf16[128,32,128]{0,2,1:T(8,128)(2,1)S(1)}, u32[]{:S(2)}, u32[]{:S(2)}) async-start(bf16[128,32,128]{0,2,1:T(8,128)(2,1)} %bitcast.8), calls=%async_computation.3 | async-start | bytes 2097152 | tf_op jit(solution)/shard_map/all_to_all | solution.py:84
  298.4 19.1 %copy-start.7 = (bf16[8,4,128,1,128]{2,4,1,3,0:T(8,128)(2,1)S(1)}, bf16[8,4,128,1,128]{2,4,1,3,0:T(8,128)(2,1)}, u32[]{:S(2)}) copy-start(bf16[8,4,128,1,128]{2,4,1,3,0:T(8,128)(2,1)} %copy-done.6) | copy-start | bytes 3145732 | tf_op jit(solution)/shard_map/while
  298.4 19.1 %copy-start.9 = (bf16[8,4,128,1,128]{4,2,1,3,0:T(8,128)(2,1)S(1)}, bf16[8,4,128,1,128]{4,2,1,3,0:T(8,128)(2,1)}, u32[]{:S(2)}) copy-start(bf16[8,4,128,1,128]{4,2,1,3,0:T(8,128)(2,1)} %copy-done.8) | copy-start | bytes 3145732 | tf_op jit(solution)/shard_map/while
  355.6 18.8 %copy-start.7 = (bf16[8,4,128,1,128]{2,4,1,3,0:T(8,128)(2,1)S(1)}, bf16[8,4,128,1,128]{2,4,1,3,0:T(8,128)(2,1)}, u32[]{:S(2)}) copy-start(bf16[8,4,128,1,128]{2,4,1,3,0:T(8,128)(2,1)} %copy-done.6) | copy-start | bytes 3145732 | tf_op jit(solution)/shard_map/while
  355.6 18.8 %copy-start.9 = (bf16[8,4,128,1,128]{4,2,1,3,0:T(8,128)(2,1)S(1)}, bf16[8,4,128,1,128]{4,2,1,3,0:T(8,128)(2,1)}, u32[]{:S(2)}) copy-start(bf16[8,4,128,1,128]{4,2,1,3,0:T(8,128)(2,1)} %copy-done.8) | copy-start | bytes 3145732 | tf_op jit(solution)/shard_map/while
  469.3 18.8 %copy-start.7 = (bf16[8,4,128,1,128]{2,4,1,3,0:T(8,128)(2,1)S(1)}, bf16[8,4,128,1,128]{2,4,1,3,0:T(8,128)(2,1)}, u32[]{:S(2)}) copy-start(bf16[8,4,128,1,128]{2,4,1,3,0:T(8,128)(2,1)} %copy-done.6) | copy-start | bytes 3145732 | tf_op jit(solution)/shard_map/while
  469.3 18.8 %copy-start.9 = (bf16[8,4,128,1,128]{4,2,1,3,0:T(8,128)(2,1)S(1)}, bf16[8,4,128,1,128]{4,2,1,3,0:T(8,128)(2,1)}, u32[]{:S(2)}) copy-start(bf16[8,4,128,1,128]{4,2,1,3,0:T(8,128)(2,1)} %copy-done.8) | copy-start | bytes 3145732 | tf_op jit(solution)/shard_map/while
  639.6 19.2 %copy-start.7 = (bf16[8,4,128,1,128]{2,4,1,3,0:T(8,128)(2,1)S(1)}, bf16[8,4,128,1,128]{2,4,1,3,0:T(8,128)(2,1)}, u32[]{:S(2)}) copy-start(bf16[8,4,128,1,128]{2,4,1,3,0:T(8,128)(2,1)} %copy-done.6) | copy-start | bytes 3145732 | tf_op jit(solution)/shard_map/while
  639.6 19.2 %copy-start.9 = (bf16[8,4,128,1,128]{4,2,1,3,0:T(8,128)(2,1)S(1)}, bf16[8,4,128,1,128]{4,2,1,3,0:T(8,128)(2,1)}, u32[]{:S(2)}) copy-start(bf16[8,4,128,1,128]{4,2,1,3,0:T(8,128)(2,1)} %copy-done.8) | copy-start | bytes 3145732 | tf_op jit(solution)/shard_map/while
  673.5 45.3 %collective-permute-start.4 = (bf16[2,4096,128]{2,1,0:T(8,128)(2,1)}, bf16[2,4096,128]{2,1,0:T(8,128)(2,1)S(1)}, u32[]{:S(2)}, u32[]{:S(2)}) collective-permute-start(bf16[2,4096,128]{2,1,0:T(8,128)(2,1)} %get-tuple-element.109), channel_id=1, source_target_pairs={{64,0},{96,32},{128,64},{160,96},{192,128},{224,160},{65,1},{97,33... | collective-permute-start | bytes 6291464 | tf_op jit(solution)/shard_map/ppermute | solution.py:13
  675.4 50.8 %collective-permute-start.7 = (bf16[2,4096,128]{2,1,0:T(8,128)(2,1)}, bf16[2,4096,128]{2,1,0:T(8,128)(2,1)}, u32[]{:S(2)}, u32[]{:S(2)}) collective-permute-start(bf16[2,4096,128]{2,1,0:T(8,128)(2,1)} %get-tuple-element.110), channel_id=1, source_target_pairs={{0,64},{32,96},{64,128},{96,160},{128,192},{160,224},{1,65},{33,97... | collective-permute-start | bytes 6291464 | tf_op jit(solution)/shard_map/ppermute | solution.py:13
  679.3 64.0 %collective-permute-start.6 = (bf16[2,4096,128]{2,1,0:T(8,128)(2,1)}, bf16[2,4096,128]{2,1,0:T(8,128)(2,1)}, u32[]{:S(2)}, u32[]{:S(2)}) collective-permute-start(bf16[2,4096,128]{2,1,0:T(8,128)(2,1)} %get-tuple-element.111), channel_id=1, source_target_pairs={{0,32},{32,64},{64,96},{96,128},{128,160},{160,192},{192,224},{1,3... | collective-permute-start | bytes 6291464 | tf_op jit(solution)/shard_map/ppermute | solution.py:13
  681.2 62.1 %collective-permute-start.5 = (bf16[2,4096,128]{2,1,0:T(8,128)(2,1)}, bf16[2,4096,128]{2,1,0:T(8,128)(2,1)}, u32[]{:S(2)}, u32[]{:S(2)}) collective-permute-start(bf16[2,4096,128]{2,1,0:T(8,128)(2,1)} %get-tuple-element.112), channel_id=1, source_target_pairs={{32,0},{64,32},{96,64},{128,96},{160,128},{192,160},{224,192},{33,... | collective-permute-start | bytes 6291464 | tf_op jit(solution)/shard_map/ppermute | solution.py:13
  684.9 64.4 %all-to-all-start.4 = ((bf16[32,128,128]{2,1,0:T(8,128)(2,1)}), bf16[32,128,128]{2,1,0:T(8,128)(2,1)S(1)}, u32[]{:S(2)}, u32[]{:S(2)}) async-start(bf16[32,128,128]{2,1,0:T(8,128)(2,1)} %bitcast.198), calls=%async_computation.4 | async-start | bytes 2097152 | tf_op jit(solution)/shard_map/all_to_all | solution.py:119
  786.3 33.2 %all-to-all-start.6 = ((bf16[32,128,128]{2,1,0:T(8,128)(2,1)}), bf16[32,128,128]{2,1,0:T(8,128)(2,1)S(1)}, u32[]{:S(2)}, u32[]{:S(2)}) async-start(bf16[32,128,128]{2,1,0:T(8,128)(2,1)} %bitcast.196), calls=%async_computation.6 | async-start | bytes 2097152 | tf_op jit(solution)/shard_map/all_to_all | solution.py:121
  794.8 26.7 %copy-start.1 = (bf16[128,4096]{1,0:T(8,128)(2,1)S(1)}, bf16[128,4096]{1,0:T(8,128)(2,1)}, u32[]{:S(2)}) copy-start(bf16[128,4096]{1,0:T(8,128)(2,1)} %param.9) | copy-start | bytes 3145732
  (52 other events, 400.0 us)
where the time goes:
time: 825 us; the launch traced here: 822 us
  local copies, waits for them, and re-layouts  237 us (29%)
  other arithmetic  200 us (24%)
  waiting for transfers between devices  169 us (20%)
  matrix products  89.9 us (11%)
  blocking collectives  70.3 us (9%)
  starting transfers between devices  54.3 us (7%)
    scatter-add x8, other arithmetic, one_group(): totals = totals.at[:, id_group.reshape(-1)].add(update)  150 us
    ppermute x8, waiting for transfers between devices, from_behind(): return lax.ppermute(block, axis, route)  100 us
    dot_general x48, matrix products, fast_product(): jnp.einsum(pattern, first_op, second_op, preferred_element_type=jnp.float32)  89.9 us
    gather x8, local copies, waits for them, and re-layouts, one_group(): value_tiles[id_group]  38.9 us
    transpose x8, local copies, waits for them, and re-layouts, fast_product(): jnp.einsum(pattern, first_op, second_op, preferred_element_type=jnp.float32)  38.9 us
    mul x8, local copies, waits for them, and re-layouts, one_group(): product('ghqk,gqhd->gkhd', grad_scores, query_group) * score_scale  37.9 us
    all_to_all x1, blocking collectives, local(): lax.all_to_all(key_grad, 'space', split_axis=0, concat_axis=1, tiled=True)  37 us
    all_to_all x1, blocking collectives, local(): lax.all_to_all(value_rows, 'space', split_axis=1, concat_axis=0, tiled=True)  33.3 us
  transfers between devices with their start and end apart: 13, of which 9 were waited for; matrix products, arithmetic and copies ran while one was open for 5% of the time, Pallas kernels for 0%

commit v1 on v0

v1 whole, which is shorter than its diff:
```python
import jax
import jax.numpy as jnp
from jax import lax
from jax.experimental import pallas as pl
from jax.experimental.pallas import tpu as pltpu
from jax.sharding import PartitionSpec as P

HD = 128
BLK = 128
SLAB = 8
SCALE = HD**-0.5
LOG2E = 1.4426950408889634
MESH = pl.DeviceIdType.MESH

WINDOW = 48
SEGMENTS = ((0, 5, 0), (12, 3, 5), (22, 3, 8), (32, 1, 11), (40, 1, 12))
SLOTS = 13
FRAME_STEPS = (0,) * 5 + (1,) * 3 + (-1,) * 3 + (2, -2)
BLOCK_STEPS = (-2, -1, 0, 1, 2, -1, 0, 1, -1, 0, 1, 0, 0)
HALO = (
    (0, 8, 32, -2, 0),
    (0, 8, 40, 2, 0),
    (0, 8, 13, -1, 0),
    (0, 8, 23, 1, 0),
    (0, 2, 10, 0, -1),
    (6, 2, 0, 0, 1),
    (0, 1, 21, -1, -1),
    (7, 1, 12, -1, 1),
    (0, 1, 31, 1, -1),
    (7, 1, 22, 1, 1),
)
HALO_START = tuple(sum(entry[1] for entry in HALO[:at]) for at in range(len(HALO)))
HALO_BLOCKS = sum(entry[1] for entry in HALO)
RING_ORDER = (4, 3, 5, 2, 6, 1, 7)


def product(left, right, contract_left, contract_right):
    return lax.dot_general(
        left,
        right,
        (((contract_left,), (contract_right,)), ((), ())),
        preferred_element_type=jnp.float32,
    )


def fold_rows(tile, how):
    return how(tile.reshape(BLK // 8, 8, tile.shape[-1]), axis=0)


def kernel(
    frames,
    slabs,
    heads,
    bias,
    queries,
    keys,
    values,
    grads,
    grad_queries,
    grad_keys,
    grad_values,
    pairs,
    window,
    keys_t,
    totals,
    raw,
    weights,
    part_out,
    part_in,
    query_out,
    key_out,
    in_send,
    in_recv,
    halo_send,
    halo_recv,
    part_send,
    part_recv,
    out_send,
    out_recv,
):
    frame = lax.axis_index("tm")
    space = lax.axis_index("space")
    slab = space // SLAB
    place = lax.rem(space, SLAB)

    def ring(distance):
        there = lax.rem(place + distance, SLAB)
        return there, (frame, slab * SLAB + there)

    def neighbour(frame_step, slab_step):
        to_frame = lax.rem(frame + frame_step + frames, frames)
        to_slab = lax.rem(slab + slab_step + slabs, slabs)
        return (to_frame, to_slab * SLAB + place)

    def head_columns(owner, step):
        return pl.ds(pl.multiple_of((owner * heads + step) * HD, HD), HD)

    def send(source, target, send_sem, recv_sem, device):
        pltpu.make_async_remote_copy(
            src_ref=source,
            dst_ref=target,
            send_sem=send_sem,
            recv_sem=recv_sem,
            device_id=device,
            device_id_type=MESH,
        ).start()

    def wait_for(ref, sem):
        pltpu.make_async_copy(ref, ref, sem).wait()

    def start_inputs(step):
        landing = (
            pairs.at[step, place, 0:BLK, 0:HD],
            pairs.at[step, place, BLK : 2 * BLK, HD : 2 * HD],
            window.at[step, 2 + place, :, 0:HD],
            window.at[step, 2 + place, :, HD : 2 * HD],
        )
        for distance in RING_ORDER:
            there, device = ring(distance)
            for at, source in ((2, keys), (3, values), (0, queries), (1, grads)):
                columns = head_columns(there, step)
                send(source.at[:, columns], landing[at], in_send.at[step], in_recv.at[step, at], device)
        for at, source in enumerate((queries, grads, keys, values)):
            columns = head_columns(place, step)
            pltpu.make_async_copy(source.at[:, columns], landing[at], in_recv.at[step, at]).start()

    def start_halo(step):
        wait_for(window.at[step, 2:10, :, 0:HD], in_recv.at[step, 2])
        wait_for(window.at[step, 2:10, :, HD : 2 * HD], in_recv.at[step, 3])
        for at, (first, count, position, frame_step, slab_step) in enumerate(HALO):
            send(
                window.at[step, 2 + first : 2 + first + count],
                window.at[step, position : position + count],
                halo_send.at[step],
                halo_recv.at[step, at],
                neighbour(frame_step, slab_step),
            )

    def compute(step):
        wait_for(pairs.at[step, :, 0:BLK, 0:HD], in_recv.at[step, 0])
        wait_for(pairs.at[step, :, BLK : 2 * BLK, HD : 2 * HD], in_recv.at[step, 1])
        for at, (_, count, position, _, _) in enumerate(HALO):
            wait_for(window.at[step, position : position + count], halo_recv.at[step, at])

        def prepare(position, carry):
            columns = pl.ds(pl.multiple_of(position * BLK, BLK), BLK)
            keys_t[:, columns] = window[step, position, :, 0:HD].T
            totals[position] = jnp.zeros((BLK, 2 * HD), jnp.float32)
            return carry

        lax.fori_loop(0, WINDOW, prepare, 0)

        def query_block(i, carry):
            pair = pairs[step, i]
            top = jnp.full((8, BLK), -3e38, jnp.float32)
            for base, count, slot in SEGMENTS:
                tiles = window[step, pl.ds(base + i, count)].reshape(count * BLK, 2 * HD)
                both = product(tiles, pair, 1, 1)
                raw[slot * BLK : (slot + count) * BLK, :] = both
                for at in range(count):
                    highest = fold_rows(both[at * BLK : (at + 1) * BLK, 0:BLK], jnp.max)
                    top = jnp.maximum(top, highest * (SCALE * LOG2E) + bias[i, slot + at])
            top = jnp.max(top, axis=0, keepdims=True)
            total = jnp.zeros((8, BLK), jnp.float32)
            delta = jnp.zeros((8, BLK), jnp.float32)
            for slot in range(SLOTS):
                rows = slice(slot * BLK, (slot + 1) * BLK)
                power = jnp.exp2(raw[rows, 0:BLK] * (SCALE * LOG2E) + (bias[i, slot] - top))
                total = total + fold_rows(power, jnp.sum)
                delta = delta + fold_rows(power * raw[rows, BLK : 2 * BLK], jnp.sum)
                raw[rows, 0:BLK] = power
            inverse = 1.0 / jnp.sum(total, axis=0, keepdims=True)
            delta = jnp.sum(delta, axis=0, keepdims=True) * inverse
            for slot in range(SLOTS):
                rows = slice(slot * BLK, (slot + 1) * BLK)
                probs = raw[rows, 0:BLK] * inverse
                grad_scores = probs * (raw[rows, BLK : 2 * BLK] - delta)
                weights[rows, 0:BLK] = grad_scores.astype(jnp.bfloat16)
                weights[rows, BLK : 2 * BLK] = probs.astype(jnp.bfloat16)
            grad_query = jnp.zeros((HD, BLK), jnp.float32)
            for base, count, slot in SEGMENTS:
                rows = slice(slot * BLK, (slot + count) * BLK)
                columns = pl.ds(pl.multiple_of((base + i) * BLK, BLK), count * BLK)
                grad_query = grad_query + product(keys_t[:, columns], weights[rows, 0:BLK], 1, 0)
                update = product(weights[rows, :], pair, 1, 0)
                totals[pl.ds(base + i, count)] += update.reshape(count, BLK, 2 * HD)
            query_out[step, i] = (grad_query * SCALE).T.astype(jnp.bfloat16)
            return carry

        lax.fori_loop(0, SLAB, query_block, 0)

        for at, (_, count, position, frame_step, slab_step) in enumerate(HALO):
            start = HALO_START[at]
            for extra in range(count):
                round_total(totals.at[position + extra], part_out.at[step, start + extra])
            send(
                part_out.at[step, start : start + count],
                part_in.at[step, start : start + count],
                part_send.at[step],
                part_recv.at[step, at],
                neighbour(-frame_step, -slab_step),
            )
        for block in range(SLAB):
            round_total(totals.at[2 + block], key_out.at[step, block])
        start_output(step, 0, grad_queries, lambda block: query_out.at[step, block])

    def round_total(source, target):
        target[:, 0:HD] = (source[:, 0:HD] * SCALE).astype(jnp.bfloat16)
        target[:, HD : 2 * HD] = source[:, HD : 2 * HD].astype(jnp.bfloat16)

    def start_output(step, at, result, tile_of):
        target = result.at[:, head_columns(place, step)]
        for distance in RING_ORDER:
            there, device = ring(distance)
            send(tile_of(there), target, out_send.at[at], out_recv.at[at], device)
        pltpu.make_async_copy(tile_of(place), target, out_recv.at[at]).start()

    def finish(step):
        for at, (_, count, _, _, _) in enumerate(HALO):
            start = HALO_START[at]
            wait_for(part_in.at[step, start : start + count], part_recv.at[step, at])
        for block in range(SLAB):
            summed = key_out[step, block].astype(jnp.float32)
            for at, (first, count, _, _, _) in enumerate(HALO):
                if first <= block < first + count:
                    arrived = part_in[step, HALO_START[at] + block - first]
                    summed = summed + arrived.astype(jnp.float32)
            key_out[step, block] = summed.astype(jnp.bfloat16)
        start_output(step, 1, grad_keys, lambda block: key_out.at[step, block, :, 0:HD])
        start_output(step, 2, grad_values, lambda block: key_out.at[step, block, :, HD : 2 * HD])

    barrier = pltpu.get_barrier_semaphore()
    for distance in range(1, SLAB):
        pl.semaphore_signal(barrier, inc=1, device_id=ring(distance)[1], device_id_type=MESH)
    for _, _, _, frame_step, slab_step in HALO:
        device = neighbour(frame_step, slab_step)
        pl.semaphore_signal(barrier, inc=1, device_id=device, device_id_type=MESH)
    zeros = jnp.zeros((BLK, HD), jnp.bfloat16)

    def clear(at, carry):
        step, block = at // SLAB, lax.rem(at, SLAB)
        pairs[step, block, 0:BLK, HD : 2 * HD] = zeros
        pairs[step, block, BLK : 2 * BLK, 0:HD] = zeros
        return carry

    lax.fori_loop(0, heads * SLAB, clear, 0)
    pl.semaphore_wait(barrier, SLAB - 1 + len(HALO))

    start_inputs(0)
    start_inputs(1)

    def stage(at, carry):
        @pl.when(at < heads)
        def _():
            start_halo(at)

        @pl.when(at + 2 < heads)
        def _():
            start_inputs(at + 2)

        @pl.when((at >= 1) & (at < heads + 1))
        def _():
            compute(at - 1)

        @pl.when(at >= 2)
        def _():
            finish(at - 2)

        return carry

    lax.fori_loop(0, heads + 2, stage, 0)

    for at, result in enumerate((grad_queries, grad_keys, grad_values)):
        wait_for(result, out_recv.at[at])
    sent_tiles = (SLAB - 1) * heads // 2
    for at in range(3):
        wait_for(window.at[0, 0:sent_tiles], out_send.at[at])

    def drain(step, carry):
        wait_for(window.at[step, 0 : (SLAB - 1) * 2], in_send.at[step])
        wait_for(window.at[step, 0:HALO_BLOCKS], halo_send.at[step])
        wait_for(part_in.at[step], part_send.at[step])
        return carry

    lax.fori_loop(0, heads, drain, 0)


def live_bias(block_lists, block_counts, frames):
    frame = lax.axis_index("tm")
    slab = lax.axis_index("space") // SLAB
    frame_blocks = block_lists.shape[1]
    lists = lax.dynamic_slice_in_dim(block_lists[0], slab * SLAB, SLAB, 0)
    counts = lax.dynamic_slice_in_dim(block_counts[0], slab * SLAB, SLAB, 0)
    to_frame = frame + jnp.array(FRAME_STEPS, jnp.int32)[None, :]
    to_block = slab * SLAB + jnp.arange(SLAB)[:, None] + jnp.array(BLOCK_STEPS, jnp.int32)[None, :]
    inside = (to_frame >= 0) & (to_frame < frames) & (to_block >= 0) & (to_block < frame_blocks)
    wanted = to_frame * frame_blocks + to_block
    listed = jnp.arange(lists.shape[1])[None, :] < counts[:, None]
    named = (lists[:, None, :] == wanted[:, :, None]) & listed[:, None, :]
    return jnp.where(inside & jnp.any(named, axis=-1), 0.0, -1e30).astype(jnp.float32)


def solution(mesh):
    frames = mesh.shape["tm"]
    slabs = mesh.shape["space"] // SLAB

    def local(queries, key_rows, value_rows, grads_out, block_lists, block_counts):
        bias = live_bias(block_lists, block_counts, frames)
        rows, width = queries.shape
        heads = width // HD // SLAB
        shape = jax.ShapeDtypeStruct((rows, width), jnp.bfloat16)
        anywhere = pl.BlockSpec(memory_space=pl.ANY)

        def body(*refs):
            kernel(frames, slabs, heads, *refs)

        return pl.pallas_call(
            body,
            out_shape=(shape, shape, shape),
            in_specs=[pl.BlockSpec(memory_space=pltpu.SMEM)] + [anywhere] * 4,
            out_specs=(anywhere, anywhere, anywhere),
            scratch_shapes=[
                pltpu.VMEM((heads, SLAB, 2 * BLK, 2 * HD), jnp.bfloat16),
                pltpu.VMEM((heads, WINDOW, BLK, 2 * HD), jnp.bfloat16),
                pltpu.VMEM((HD, WINDOW * BLK), jnp.bfloat16),
                pltpu.VMEM((WINDOW, BLK, 2 * HD), jnp.float32),
                pltpu.VMEM((SLOTS * BLK, 2 * BLK), jnp.float32),
                pltpu.VMEM((SLOTS * BLK, 2 * BLK), jnp.bfloat16),
                pltpu.VMEM((heads, HALO_BLOCKS, BLK, 2 * HD), jnp.bfloat16),
                pltpu.VMEM((heads, HALO_BLOCKS, BLK, 2 * HD), jnp.bfloat16),
                pltpu.VMEM((heads, SLAB, BLK, HD), jnp.bfloat16),
                pltpu.VMEM((heads, SLAB, BLK, 2 * HD), jnp.bfloat16),
                pltpu.SemaphoreType.DMA((heads,)),
                pltpu.SemaphoreType.DMA((heads, 4)),
                pltpu.SemaphoreType.DMA((heads,)),
                pltpu.SemaphoreType.DMA((heads, len(HALO))),
                pltpu.SemaphoreType.DMA((heads,)),
                pltpu.SemaphoreType.DMA((heads, len(HALO))),
                pltpu.SemaphoreType.DMA((3,)),
                pltpu.SemaphoreType.DMA((3,)),
            ],
            compiler_params=pltpu.CompilerParams(
                collective_id=0, has_side_effects=True, vmem_limit_bytes=60 * 1024 * 1024
            ),
        )(bias, queries, key_rows, value_rows, grads_out)

    rows = P(("tm", "space"), None)
    return jax.shard_map(
        local,
        mesh=mesh,
        in_specs=(rows, rows, rows, rows, P("tm", None, None), P("tm", None)),
        out_specs=(rows, rows, rows),
        check_vma=False,
    )
```

time: 825 us -> 214 us (0.26)
  local copies, waits for them, and re-layouts: 237 us -> 7.24 us
  Pallas kernels: 0 us -> 205 us
  other arithmetic: 200 us -> 1.23 us
  waiting for transfers between devices: 169 us -> 0 us
  matrix products: 89.9 us -> 0 us
  blocking collectives: 70.3 us -> 0 us
  starting transfers between devices: 54.3 us -> 0 us
    pallas_call x0 -> x1, Pallas kernels: none -> 205 us  [local(): pl.pallas_call(body, out_shape=(shape, shape, shape), in_specs=[pl.BlockS...]
    scatter-add x8 -> x0, other arithmetic: 150 us -> none  [one_group(): totals = totals.at[:, id_group.reshape(-1)].add(update)]
    ppermute x8 -> x0, waiting for transfers between devices: 100 us -> none  [from_behind(): return lax.ppermute(block, axis, route)]
    dot_general x48 -> x0, matrix products: 89.9 us -> none  [fast_product(): jnp.einsum(pattern, first_op, second_op, preferred_element_type=jnp.float32)]
    all_to_all x2 -> x0, blocking collectives: 70.3 us -> none  [the longest x1 37 us: local(): lax.all_to_all(key_grad, 'space', split_axis=0, concat_axis=1, tiled=True)]
    all_to_all x5 -> x0, waiting for transfers between devices: 68.4 us -> none  [the longest x1 28.3 us: local(): lax.all_to_all(key_rows, 'space', split_axis=1, concat_axis=0, tiled=True)]
    gather x16 -> x0, local copies, waits for them, and re-layouts: 65.8 us -> none  [the longest x8 38.9 us: one_group(): value_tiles[id_group]]
    transpose x8 -> x0, local copies, waits for them, and re-layouts: 38.9 us -> none  [fast_product(): jnp.einsum(pattern, first_op, second_op, preferred_element_type=jnp.float32)]
  transfers between devices with their start and end apart: 13 -> 0, of which waited for: 9 -> 0; matrix products, arithmetic and copies ran while one was open for 5% -> 0% of each run, Pallas kernels for 0% -> 0%
where the time goes in v1:
time: 214 us
  Pallas kernels  205 us (96%)
  local copies, waits for them, and re-layouts  7.24 us (3%)
    pallas_call x1, Pallas kernels, local(): pl.pallas_call(body, out_shape=(shape, shape, shape), in_specs=[pl.BlockS...  205 us
    unnamed x16, local copies, waits for them, and re-layouts  6.91 us

profile of v1, /device:TPU:2, one launch (start us, length us, event | category | flops | bytes accessed | tf_op | source)
XLA Modules:
  0.0 213.8 jit_solution(10874697120779418607)
XLA Ops:
  0.6 0.0 copy-start
  0.7 0.0 copy-start.4
  0.7 0.6 copy-done.4
  1.3 0.1 dynamic-slice_bitcast_fusion
  1.4 0.0 copy-start.5
  1.4 0.1 iota_compare_fusion
  1.5 0.6 copy-done.5
  2.1 0.0 copy-start.3
  2.1 0.6 copy-done.3
  2.7 0.1 add_add_fusion
  2.8 0.1 copy.13
  2.9 0.0 copy-done
  2.9 0.1 constant_dynamic-slice_fusion
  3.0 0.1 copy.15
  3.0 0.4 and_reduce_fusion
  3.4 0.1 copy.14
  3.5 0.7 fusion.3.refs_0_
  4.2 204.6 %shard_map.103 = (bf16[128,4096]{1,0:T(8,128)(2,1)}, bf16[128,4096]{1,0:T(8,128)(2,1)}, bf16[128,4096]{1,0:T(8,128)(2,1)}) custom-call(f32[8,13]{1,0:T(8,128)} %fusion.3.refs_0_, bf16[128,4096]{1,0:T(8,128)(2,1)} %refs_1_.1, bf16[128,4096]{1,0:T(8,128)(2,1)} %refs_2_.1, bf16[128,4096]{1,0:T(8,128)(2,1)} %refs_3_.1, bf16[128,4096]{1,0:T(8,128)(2,1)} %refs_4_.1), custom_call_target="tpu_custom_call" | custom-call | tf_op jit(solution)/shard_map/pallas_call | solution.py:317
  208.8 0.0 copy-start.2
  208.8 2.4 %copy.19 = bf16[128,4096]{1,0:T(8,128)(2,1)} copy(bf16[128,4096]{1,0:T(8,128)(2,1)} %get-tuple-element.6) | data formatting | bytes 2097152
  211.2 0.0 copy-done.2
  211.2 1.0 copy.20
  212.2 0.6 copy-done.1
  212.8 1.0 copy.21
  (4 shorter events, 0.0 us)
Async XLA Ops:
  0.6 2.2 %copy-start = (s32[1,32,13]{1,0,2:T(1,128)S(1)}, s32[1,32,13]{1,0,2:T(1,128)}, u32[]{:S(2)}) copy-start(s32[1,32,13]{1,0,2:T(1,128)} %param.12) | copy-start | bytes 4996
  0.7 0.7 copy-start.4
  1.4 0.7 copy-start.5
  2.1 0.7 copy-start.3
  208.8 2.4 %copy-start.2 = (bf16[128,4096]{1,0:T(8,128)(2,1)S(1)}, bf16[128,4096]{1,0:T(8,128)(2,1)}, u32[]{:S(2)}) copy-start(bf16[128,4096]{1,0:T(8,128)(2,1)} %get-tuple-element.7) | copy-start | bytes 3145732
  211.2 1.6 copy-start.1

commit v2 on v1

--- a/solution.py
+++ b/solution.py
@@ -17,11 +17,14 @@
 SLOTS = 13
 FRAME_STEPS = (0,) * 5 + (1,) * 3 + (-1,) * 3 + (2, -2)
 BLOCK_STEPS = (-2, -1, 0, 1, 2, -1, 0, 1, -1, 0, 1, 0, 0)
-HALO = (
-    (0, 8, 32, -2, 0),
-    (0, 8, 40, 2, 0),
-    (0, 8, 13, -1, 0),
-    (0, 8, 23, 1, 0),
+OUTER, OUTER2, INNER, INNER2 = range(4)
+
+
+def whole_frame(which, outward):
+    return (18 - 5 * outward, 36 - 4 * outward, 18 + 5 * outward, 36 + 4 * outward)[which]
+
+
+EDGES = (
     (0, 2, 10, 0, -1),
     (6, 2, 0, 0, 1),
     (0, 1, 21, -1, -1),
@@ -29,8 +32,10 @@
     (0, 1, 31, 1, -1),
     (7, 1, 22, 1, 1),
 )
-HALO_START = tuple(sum(entry[1] for entry in HALO[:at]) for at in range(len(HALO)))
-HALO_BLOCKS = sum(entry[1] for entry in HALO)
+EDGE_START = tuple(24 + sum(entry[1] for entry in EDGES[:at]) for at in range(len(EDGES)))
+JOIN = 32
+HALO_BLOCKS = 40
+PEERS = 4 + len(EDGES)
 RING_ORDER = (4, 3, 5, 2, 6, 1, 7)
 
 
@@ -51,7 +56,8 @@
     frames,
     slabs,
     heads,
-    bias,
+    block_lists,
+    block_counts,
     queries,
     keys,
     values,
@@ -65,6 +71,7 @@
     totals,
     raw,
     weights,
+    bias,
     part_out,
     part_in,
     query_out,
@@ -82,6 +89,7 @@
     space = lax.axis_index("space")
     slab = space // SLAB
     place = lax.rem(space, SLAB)
+    outward = 2 * lax.rem(frame, 2) - 1
 
     def ring(distance):
         there = lax.rem(place + distance, SLAB)
@@ -127,20 +135,34 @@
     def start_halo(step):
         wait_for(window.at[step, 2:10, :, 0:HD], in_recv.at[step, 2])
         wait_for(window.at[step, 2:10, :, HD : 2 * HD], in_recv.at[step, 3])
-        for at, (first, count, position, frame_step, slab_step) in enumerate(HALO):
+        own = window.at[step, 2:10]
+        for which, distance, there in ((OUTER, 1, -outward), (OUTER2, -2, outward), (INNER, -1, -outward)):
+            target = window.at[step, pl.ds(whole_frame(which, there), SLAB)]
+            device = neighbour(distance * outward, 0)
+            send(own, target, halo_send.at[step], halo_recv.at[step, which], device)
+        for at, (first, count, position, frame_step, slab_step) in enumerate(EDGES):
             send(
                 window.at[step, 2 + first : 2 + first + count],
                 window.at[step, position : position + count],
                 halo_send.at[step],
-                halo_recv.at[step, at],
+                halo_recv.at[step, 4 + at],
                 neighbour(frame_step, slab_step),
             )
+
+    def pass_halo(step):
+        arrived = window.at[step, pl.ds(whole_frame(OUTER, outward), SLAB)]
+        wait_for(arrived, halo_recv.at[step, OUTER])
+        target = window.at[step, pl.ds(whole_frame(INNER2, -outward), SLAB)]
+        send(arrived, target, halo_send.at[step], halo_recv.at[step, INNER2], neighbour(-outward, 0))
 
     def compute(step):
         wait_for(pairs.at[step, :, 0:BLK, 0:HD], in_recv.at[step, 0])
         wait_for(pairs.at[step, :, BLK : 2 * BLK, HD : 2 * HD], in_recv.at[step, 1])
-        for at, (_, count, position, _, _) in enumerate(HALO):
-            wait_for(window.at[step, position : position + count], halo_recv.at[step, at])
+        for which in (OUTER2, INNER, INNER2):
+            arrived = window.at[step, pl.ds(whole_frame(which, outward), SLAB)]
+            wait_for(arrived, halo_recv.at[step, which])
+        for at, (_, count, position, _, _) in enumerate(EDGES):
+            wait_for(window.at[step, position : position + count], halo_recv.at[step, 4 + at])
 
         def prepare(position, carry):
             columns = pl.ds(pl.multiple_of(position * BLK, BLK), BLK)
@@ -151,6 +173,26 @@
         lax.fori_loop(0, WINDOW, prepare, 0)
 
         def query_block(i, carry):
+            @pl.when((i == 1) & (step >= 1))
+            def _():
+                join_parts(step - 1)
+
+            @pl.when((i == 2) & (step + 1 < heads))
+            def _():
+                start_halo(step + 1)
+
+            @pl.when((i == 2) & (step + 3 < heads))
+            def _():
+                start_inputs(step + 3)
+
+            @pl.when((i == 6) & (step + 1 < heads))
+            def _():
+                pass_halo(step + 1)
+
+            @pl.when((i == 7) & (step >= 1))
+            def _():
+                finish(step - 1)
+
             pair = pairs[step, i]
             top = jnp.full((8, BLK), -3e38, jnp.float32)
             for base, count, slot in SEGMENTS:
@@ -189,20 +231,52 @@
 
         lax.fori_loop(0, SLAB, query_block, 0)
 
-        for at, (_, count, position, frame_step, slab_step) in enumerate(HALO):
-            start = HALO_START[at]
+        def round_frame(which, start):
+            def one(block, carry):
+                round_total(totals.at[whole_frame(which, outward) + block], part_out.at[step, start + block])
+                return carry
+
+            lax.fori_loop(0, SLAB, one, 0)
+
+        round_frame(INNER2, JOIN)
+        send_part(step, JOIN, SLAB, INNER2, neighbour(-outward, 0))
+        round_frame(OUTER2, 2 * SLAB)
+        send_part(step, 2 * SLAB, SLAB, OUTER2, neighbour(2 * outward, 0))
+        for at, (_, count, position, frame_step, slab_step) in enumerate(EDGES):
             for extra in range(count):
-                round_total(totals.at[position + extra], part_out.at[step, start + extra])
-            send(
-                part_out.at[step, start : start + count],
-                part_in.at[step, start : start + count],
-                part_send.at[step],
-                part_recv.at[step, at],
-                neighbour(-frame_step, -slab_step),
-            )
-        for block in range(SLAB):
+                round_total(totals.at[position + extra], part_out.at[step, EDGE_START[at] + extra])
+            send_part(step, EDGE_START[at], count, 4 + at, neighbour(-frame_step, -slab_step))
+        round_frame(INNER, 0)
+        send_part(step, 0, SLAB, INNER, neighbour(-outward, 0))
+        round_frame(OUTER, SLAB)
+
+        def round_own(block, carry):
             round_total(totals.at[2 + block], key_out.at[step, block])
+            return carry
+
+        lax.fori_loop(0, SLAB, round_own, 0)
         start_output(step, 0, grad_queries, lambda block: query_out.at[step, block])
+
+    def send_part(step, start, count, at, device):
+        send(
+            part_out.at[step, start : start + count],
+            part_in.at[step, start : start + count],
+            part_send.at[step],
+            part_recv.at[step, at],
+            device,
+        )
+
+    def join_parts(step):
+        wait_for(part_in.at[step, JOIN : JOIN + SLAB], part_recv.at[step, INNER2])
+
+        def one(block, carry):
+            mine = part_out[step, SLAB + block].astype(jnp.float32)
+            other = part_in[step, JOIN + block].astype(jnp.float32)
+            part_out[step, SLAB + block] = (mine + other).astype(jnp.bfloat16)
+            return carry
+
+        lax.fori_loop(0, SLAB, one, 0)
+        send_part(step, SLAB, SLAB, OUTER, neighbour(outward, 0))
 
     def round_total(source, target):
         target[:, 0:HD] = (source[:, 0:HD] * SCALE).astype(jnp.bfloat16)
@@ -216,23 +290,48 @@
         pltpu.make_async_copy(tile_of(place), target, out_recv.at[at]).start()
 
     def finish(step):
-        for at, (_, count, _, _, _) in enumerate(HALO):
-            start = HALO_START[at]
-            wait_for(part_in.at[step, start : start + count], part_recv.at[step, at])
+        for at, start in ((INNER, 0), (OUTER, SLAB), (OUTER2, 2 * SLAB)):
+            wait_for(part_in.at[step, start : start + SLAB], part_recv.at[step, at])
+        for at, (_, count, _, _, _) in enumerate(EDGES):
+            start = EDGE_START[at]
+            wait_for(part_in.at[step, start : start + count], part_recv.at[step, 4 + at])
         for block in range(SLAB):
             summed = key_out[step, block].astype(jnp.float32)
-            for at, (first, count, _, _, _) in enumerate(HALO):
+            for start in (0, SLAB, 2 * SLAB):
+                summed = summed + part_in[step, start + block].astype(jnp.float32)
+            for at, (first, count, _, _, _) in enumerate(EDGES):
                 if first <= block < first + count:
-                    arrived = part_in[step, HALO_START[at] + block - first]
+                    arrived = part_in[step, EDGE_START[at] + block - first]
                     summed = summed + arrived.astype(jnp.float32)
             key_out[step, block] = summed.astype(jnp.bfloat16)
         start_output(step, 1, grad_keys, lambda block: key_out.at[step, block, :, 0:HD])
         start_output(step, 2, grad_values, lambda block: key_out.at[step, block, :, HD : 2 * HD])
 
+    def find_bias():
+        frame_blocks, listed = block_lists.shape[1], block_lists.shape[2]
+
+        def one(i, carry):
+            block = slab * SLAB + i
+            count = block_counts[0, block]
+            named = [jnp.where(at < count, block_lists[0, block, at], -1) for at in range(listed)]
+            for slot in range(SLOTS):
+                to_frame, to_block = frame + FRAME_STEPS[slot], block + BLOCK_STEPS[slot]
+                wanted = to_frame * frame_blocks + to_block
+                inside = (to_frame >= 0) & (to_frame < frames) & (to_block >= 0) & (to_block < frame_blocks)
+                wanted = jnp.where(inside, wanted, -2)
+                live = named[0] == wanted
+                for entry in named[1:]:
+                    live = live | (entry == wanted)
+                bias[i, slot] = jnp.where(live, jnp.float32(0), jnp.float32(-1e30))
+            return carry
+
+        lax.fori_loop(0, SLAB, one, 0)
+
     barrier = pltpu.get_barrier_semaphore()
     for distance in range(1, SLAB):
         pl.semaphore_signal(barrier, inc=1, device_id=ring(distance)[1], device_id_type=MESH)
-    for _, _, _, frame_step, slab_step in HALO:
+    steps = [(distance * outward, 0) for distance in (1, 2, -1, -2)]
+    for frame_step, slab_step in steps + [entry[3:] for entry in EDGES]:
         device = neighbour(frame_step, slab_step)
         pl.semaphore_signal(barrier, inc=1, device_id=device, device_id_type=MESH)
     zeros = jnp.zeros((BLK, HD), jnp.bfloat16)
@@ -244,31 +343,22 @@
         return carry
 
     lax.fori_loop(0, heads * SLAB, clear, 0)
-    pl.semaphore_wait(barrier, SLAB - 1 + len(HALO))
+    pl.semaphore_wait(barrier, SLAB - 1 + PEERS)
 
     start_inputs(0)
     start_inputs(1)
-
-    def stage(at, carry):
-        @pl.when(at < heads)
-        def _():
-            start_halo(at)
-
-        @pl.when(at + 2 < heads)
-        def _():
-            start_inputs(at + 2)
-
-        @pl.when((at >= 1) & (at < heads + 1))
-        def _():
-            compute(at - 1)
-
-        @pl.when(at >= 2)
-        def _():
-            finish(at - 2)
-
+    find_bias()
+    start_halo(0)
+    start_inputs(2)
+    pass_halo(0)
+
+    def stage(step, carry):
+        compute(step)
         return carry
 
-    lax.fori_loop(0, heads + 2, stage, 0)
+    lax.fori_loop(0, heads, stage, 0)
+    join_parts(heads - 1)
+    finish(heads - 1)
 
     for at, result in enumerate((grad_queries, grad_keys, grad_values)):
         wait_for(result, out_recv.at[at])
@@ -285,27 +375,11 @@
     lax.fori_loop(0, heads, drain, 0)
 
 
-def live_bias(block_lists, block_counts, frames):
-    frame = lax.axis_index("tm")
-    slab = lax.axis_index("space") // SLAB
-    frame_blocks = block_lists.shape[1]
-    lists = lax.dynamic_slice_in_dim(block_lists[0], slab * SLAB, SLAB, 0)
-    counts = lax.dynamic_slice_in_dim(block_counts[0], slab * SLAB, SLAB, 0)
-    to_frame = frame + jnp.array(FRAME_STEPS, jnp.int32)[None, :]
-    to_block = slab * SLAB + jnp.arange(SLAB)[:, None] + jnp.array(BLOCK_STEPS, jnp.int32)[None, :]
-    inside = (to_frame >= 0) & (to_frame < frames) & (to_block >= 0) & (to_block < frame_blocks)
-    wanted = to_frame * frame_blocks + to_block
-    listed = jnp.arange(lists.shape[1])[None, :] < counts[:, None]
-    named = (lists[:, None, :] == wanted[:, :, None]) & listed[:, None, :]
-    return jnp.where(inside & jnp.any(named, axis=-1), 0.0, -1e30).astype(jnp.float32)
-
-
 def solution(mesh):
     frames = mesh.shape["tm"]
     slabs = mesh.shape["space"] // SLAB
 
     def local(queries, key_rows, value_rows, grads_out, block_lists, block_counts):
-        bias = live_bias(block_lists, block_counts, frames)
         rows, width = queries.shape
         heads = width // HD // SLAB
         shape = jax.ShapeDtypeStruct((rows, width), jnp.bfloat16)
@@ -317,7 +391,7 @@
         return pl.pallas_call(
             body,
             out_shape=(shape, shape, shape),
-            in_specs=[pl.BlockSpec(memory_space=pltpu.SMEM)] + [anywhere] * 4,
+            in_specs=[pl.BlockSpec(memory_space=pltpu.SMEM)] * 2 + [anywhere] * 4,
             out_specs=(anywhere, anywhere, anywhere),
             scratch_shapes=[
                 pltpu.VMEM((heads, SLAB, 2 * BLK, 2 * HD), jnp.bfloat16),
@@ -326,6 +400,7 @@
                 pltpu.VMEM((WINDOW, BLK, 2 * HD), jnp.float32),
                 pltpu.VMEM((SLOTS * BLK, 2 * BLK), jnp.float32),
                 pltpu.VMEM((SLOTS * BLK, 2 * BLK), jnp.bfloat16),
+                pltpu.SMEM((SLAB, SLOTS), jnp.float32),
                 pltpu.VMEM((heads, HALO_BLOCKS, BLK, 2 * HD), jnp.bfloat16),
                 pltpu.VMEM((heads, HALO_BLOCKS, BLK, 2 * HD), jnp.bfloat16),
                 pltpu.VMEM((heads, SLAB, BLK, HD), jnp.bfloat16),
@@ -333,16 +408,16 @@
                 pltpu.SemaphoreType.DMA((heads,)),
                 pltpu.SemaphoreType.DMA((heads, 4)),
                 pltpu.SemaphoreType.DMA((heads,)),
-                pltpu.SemaphoreType.DMA((heads, len(HALO))),
+                pltpu.SemaphoreType.DMA((heads, PEERS)),
                 pltpu.SemaphoreType.DMA((heads,)),
-                pltpu.SemaphoreType.DMA((heads, len(HALO))),
+                pltpu.SemaphoreType.DMA((heads, PEERS)),
                 pltpu.SemaphoreType.DMA((3,)),
                 pltpu.SemaphoreType.DMA((3,)),
             ],
             compiler_params=pltpu.CompilerParams(
                 collective_id=0, has_side_effects=True, vmem_limit_bytes=60 * 1024 * 1024
             ),
-        )(bias, queries, key_rows, value_rows, grads_out)
+        )(block_lists, block_counts, queries, key_rows, value_rows, grads_out)
 
     rows = P(("tm", "space"), None)
     return jax.shard_map(

time: 214 us -> 186 us (0.87)
  Pallas kernels: 205 us -> 178 us
    pallas_call x1, Pallas kernels: 205 us -> 178 us  [local(): pl.pallas_call(body, out_shape=(shape, shape, shape), in_specs=[pl.BlockS...]
    unnamed x16 -> x8, local copies, waits for them, and re-layouts: 6.91 us -> 6.33 us
where the time goes in v2:
time: 186 us; the launch traced here: 185 us
  Pallas kernels  178 us (96%)
  local copies, waits for them, and re-layouts  6.33 us (3%)
    pallas_call x1, Pallas kernels, local(): pl.pallas_call(body, out_shape=(shape, shape, shape), in_specs=[pl.BlockS...  178 us
    unnamed x8, local copies, waits for them, and re-layouts  6.33 us

profile of v2, /device:TPU:2, one launch (start us, length us, event | category | flops | bytes accessed | tf_op | source)
XLA Modules:
  0.0 184.9 jit_solution(1042521560384779941)
XLA Ops:
  0.6 1.4 copy.9.refs_0_
  2.0 177.9 %shard_map.85 = (bf16[128,4096]{1,0:T(8,128)(2,1)}, bf16[128,4096]{1,0:T(8,128)(2,1)}, bf16[128,4096]{1,0:T(8,128)(2,1)}) custom-call(s32[1,32,13]{2,1,0:T(8,128)} %copy.9.refs_0_, s32[1,32]{1,0:T(1,128)} %refs_1_.1, bf16[128,4096]{1,0:T(8,128)(2,1)} %refs_2_.1, bf16[128,4096]{1,0:T(8,128)(2,1)} %refs_3_.1, bf16[128,4096]{1,0:T(8,128)(2,1)} %refs_4_.1, ...), custom_call_target="tpu_custom_call" | custom-call | tf_op jit(solution)/shard_map/pallas_call | solution.py:391
  179.9 0.0 copy-start.1
  179.9 2.4 %copy.13 = bf16[128,4096]{1,0:T(8,128)(2,1)} copy(bf16[128,4096]{1,0:T(8,128)(2,1)} %get-tuple-element.6) | data formatting | bytes 2097152
  182.3 0.0 copy-done.1
  182.3 0.0 copy-start
  182.3 1.0 copy.14
  183.3 0.6 copy-done
  183.9 1.0 copy.15
Async XLA Ops:
  179.9 2.4 %copy-start.1 = (bf16[128,4096]{1,0:T(8,128)(2,1)S(1)}, bf16[128,4096]{1,0:T(8,128)(2,1)}, u32[]{:S(2)}) copy-start(bf16[128,4096]{1,0:T(8,128)(2,1)} %get-tuple-element.7) | copy-start | bytes 3145732
  182.3 1.6 copy-start

commit v3 on v2

--- a/solution.py
+++ b/solution.py
@@ -32,7 +32,10 @@
     (0, 1, 31, 1, -1),
     (7, 1, 22, 1, 1),
 )
-EDGE_START = tuple(24 + sum(entry[1] for entry in EDGES[:at]) for at in range(len(EDGES)))
+EDGE_AT = 24
+HALF = SLAB // 2
+OWN_WINDOW = 32
+PART_COPIES = 8 + len(EDGES)
 JOIN = 32
 HALO_BLOCKS = 40
 PEERS = 4 + len(EDGES)
@@ -71,6 +74,7 @@
     totals,
     raw,
     weights,
+    sums,
     bias,
     part_out,
     part_in,
@@ -90,6 +94,7 @@
     slab = space // SLAB
     place = lax.rem(space, SLAB)
     outward = 2 * lax.rem(frame, 2) - 1
+    backward = lax.rem(slab, 2)
 
     def ring(distance):
         there = lax.rem(place + distance, SLAB)
@@ -167,32 +172,41 @@
         def prepare(position, carry):
             columns = pl.ds(pl.multiple_of(position * BLK, BLK), BLK)
             keys_t[:, columns] = window[step, position, :, 0:HD].T
+            return carry
+
+        def clear_total(position, carry):
             totals[position] = jnp.zeros((BLK, 2 * HD), jnp.float32)
             return carry
 
         lax.fori_loop(0, WINDOW, prepare, 0)
-
-        def query_block(i, carry):
-            @pl.when((i == 1) & (step >= 1))
-            def _():
-                join_parts(step - 1)
-
-            @pl.when((i == 2) & (step + 1 < heads))
+        lax.fori_loop(0, OWN_WINDOW, clear_total, 0)
+
+        def query_block(turn, carry):
+            @pl.when((turn == 2) & (step >= 1))
+            def _():
+                join_parts(step - 1, 1 - backward)
+
+            @pl.when((turn == 2) & (step + 1 < heads))
             def _():
                 start_halo(step + 1)
 
-            @pl.when((i == 2) & (step + 3 < heads))
+            @pl.when((turn == 2) & (step + 3 < heads))
             def _():
                 start_inputs(step + 3)
 
-            @pl.when((i == 6) & (step + 1 < heads))
+            @pl.when((turn == 3) & (step >= 1))
+            def _():
+                finish(step - 1, backward)
+
+            @pl.when((turn == 5) & (step >= 1))
+            def _():
+                finish(step - 1, 1 - backward)
+
+            @pl.when((turn == 6) & (step + 1 < heads))
             def _():
                 pass_halo(step + 1)
 
-            @pl.when((i == 7) & (step >= 1))
-            def _():
-                finish(step - 1)
-
+            i = turn + backward * (SLAB - 1 - 2 * turn)
             pair = pairs[step, i]
             top = jnp.full((8, BLK), -3e38, jnp.float32)
             for base, count, slot in SEGMENTS:
@@ -225,87 +239,114 @@
                 columns = pl.ds(pl.multiple_of((base + i) * BLK, BLK), count * BLK)
                 grad_query = grad_query + product(keys_t[:, columns], weights[rows, 0:BLK], 1, 0)
                 update = product(weights[rows, :], pair, 1, 0)
-                totals[pl.ds(base + i, count)] += update.reshape(count, BLK, 2 * HD)
+                if base < OWN_WINDOW:
+                    totals[pl.ds(base + i, count)] += update.reshape(count, BLK, 2 * HD)
+                else:
+                    start = EDGE_AT - SLAB * outward if base == 32 else EDGE_AT + SLAB * outward
+                    part_out[step, start + i, :, 0:HD] = (update[:, 0:HD] * SCALE).astype(jnp.bfloat16)
+                    part_out[step, start + i, :, HD : 2 * HD] = update[:, HD : 2 * HD].astype(jnp.bfloat16)
             query_out[step, i] = (grad_query * SCALE).T.astype(jnp.bfloat16)
+            give(step, 0, grad_queries, query_out.at[step, i], i)
+
+            @pl.when(turn == HALF - 1)
+            def _():
+                send_far(step, backward)
+
+            @pl.when(turn == HALF + 1)
+            def _():
+                send_near(step, backward, 1 - backward)
+                join_parts(step, backward)
+
             return carry
 
         lax.fori_loop(0, SLAB, query_block, 0)
 
-        def round_frame(which, start):
-            def one(block, carry):
-                round_total(totals.at[whole_frame(which, outward) + block], part_out.at[step, start + block])
-                return carry
-
-            lax.fori_loop(0, SLAB, one, 0)
-
-        round_frame(INNER2, JOIN)
-        send_part(step, JOIN, SLAB, INNER2, neighbour(-outward, 0))
-        round_frame(OUTER2, 2 * SLAB)
-        send_part(step, 2 * SLAB, SLAB, OUTER2, neighbour(2 * outward, 0))
-        for at, (_, count, position, frame_step, slab_step) in enumerate(EDGES):
-            for extra in range(count):
-                round_total(totals.at[position + extra], part_out.at[step, EDGE_START[at] + extra])
-            send_part(step, EDGE_START[at], count, 4 + at, neighbour(-frame_step, -slab_step))
-        round_frame(INNER, 0)
-        send_part(step, 0, SLAB, INNER, neighbour(-outward, 0))
-        round_frame(OUTER, SLAB)
-
-        def round_own(block, carry):
-            round_total(totals.at[2 + block], key_out.at[step, block])
-            return carry
-
-        lax.fori_loop(0, SLAB, round_own, 0)
-        start_output(step, 0, grad_queries, lambda block: query_out.at[step, block])
+        send_far(step, 1 - backward)
+        send_near(step, 1 - backward, backward)
 
     def send_part(step, start, count, at, device):
         send(
-            part_out.at[step, start : start + count],
-            part_in.at[step, start : start + count],
+            part_out.at[step, pl.ds(start, count)],
+            part_in.at[step, pl.ds(start, count)],
             part_send.at[step],
             part_recv.at[step, at],
             device,
         )
 
-    def join_parts(step):
-        wait_for(part_in.at[step, JOIN : JOIN + SLAB], part_recv.at[step, INNER2])
-
-        def one(block, carry):
+    def send_far(step, half):
+        send_part(step, JOIN + HALF * half, HALF, 2 * INNER2 + half, neighbour(-outward, 0))
+        send_part(step, 2 * SLAB + HALF * half, HALF, 2 * OUTER2 + half, neighbour(2 * outward, 0))
+
+    def send_near(step, half, side):
+        outer, inner = whole_frame(OUTER, outward), whole_frame(INNER, outward)
+
+        def one(at, carry):
+            block = HALF * half + at
+            round_total(totals.at[outer + block], part_out.at[step, SLAB + block])
+            round_total(totals.at[inner + block], part_out.at[step, block])
+            round_total(totals.at[2 + block], key_out.at[step, block])
+            return carry
+
+        lax.fori_loop(0, HALF, one, 0)
+        send_part(step, HALF * half, HALF, 2 * INNER + half, neighbour(-outward, 0))
+        for at, count, position, start, frame_step in (
+            (8, 2, 10 - 10 * side, EDGE_AT + 2 * side, 0),
+            (10, 1, 21 - 9 * side, EDGE_AT + 4 + side, 1),
+            (12, 1, 31 - 9 * side, EDGE_AT + 6 + side, -1),
+        ):
+            for extra in range(count):
+                round_total(totals.at[position + extra], part_out.at[step, start + extra])
+            send_part(step, start, count, at + side, neighbour(frame_step, 1 - 2 * side))
+
+    def join_parts(step, half):
+        wait_for(part_in.at[step, pl.ds(JOIN + HALF * half, HALF)], part_recv.at[step, 2 * INNER2 + half])
+
+        def one(at, carry):
+            block = HALF * half + at
             mine = part_out[step, SLAB + block].astype(jnp.float32)
             other = part_in[step, JOIN + block].astype(jnp.float32)
             part_out[step, SLAB + block] = (mine + other).astype(jnp.bfloat16)
             return carry
 
-        lax.fori_loop(0, SLAB, one, 0)
-        send_part(step, SLAB, SLAB, OUTER, neighbour(outward, 0))
+        lax.fori_loop(0, HALF, one, 0)
+        send_part(step, SLAB + HALF * half, HALF, 2 * OUTER + half, neighbour(outward, 0))
 
     def round_total(source, target):
         target[:, 0:HD] = (source[:, 0:HD] * SCALE).astype(jnp.bfloat16)
         target[:, HD : 2 * HD] = source[:, HD : 2 * HD].astype(jnp.bfloat16)
 
-    def start_output(step, at, result, tile_of):
+    def give(step, at, result, tile, there):
         target = result.at[:, head_columns(place, step)]
-        for distance in RING_ORDER:
-            there, device = ring(distance)
-            send(tile_of(there), target, out_send.at[at], out_recv.at[at], device)
-        pltpu.make_async_copy(tile_of(place), target, out_recv.at[at]).start()
-
-    def finish(step):
+
+        @pl.when(there == place)
+        def _():
+            pltpu.make_async_copy(tile, target, out_recv.at[at]).start()
+
+        @pl.when(there != place)
+        def _():
+            send(tile, target, out_send.at[at], out_recv.at[at], (frame, slab * SLAB + there))
+
+    def finish(step, half):
         for at, start in ((INNER, 0), (OUTER, SLAB), (OUTER2, 2 * SLAB)):
-            wait_for(part_in.at[step, start : start + SLAB], part_recv.at[step, at])
-        for at, (_, count, _, _, _) in enumerate(EDGES):
-            start = EDGE_START[at]
-            wait_for(part_in.at[step, start : start + count], part_recv.at[step, 4 + at])
-        for block in range(SLAB):
+            arrived = part_in.at[step, pl.ds(start + HALF * half, HALF)]
+            wait_for(arrived, part_recv.at[step, 2 * at + half])
+        for at, count, start in ((8, 2, EDGE_AT + 2 * half), (10, 1, EDGE_AT + 4 + half), (12, 1, EDGE_AT + 6 + half)):
+            wait_for(part_in.at[step, pl.ds(start, count)], part_recv.at[step, at + half])
+        for at in range(HALF):
+            block = HALF * half + at
             summed = key_out[step, block].astype(jnp.float32)
             for start in (0, SLAB, 2 * SLAB):
                 summed = summed + part_in[step, start + block].astype(jnp.float32)
-            for at, (first, count, _, _, _) in enumerate(EDGES):
-                if first <= block < first + count:
-                    arrived = part_in[step, EDGE_START[at] + block - first]
-                    summed = summed + arrived.astype(jnp.float32)
-            key_out[step, block] = summed.astype(jnp.bfloat16)
-        start_output(step, 1, grad_keys, lambda block: key_out.at[step, block, :, 0:HD])
-        start_output(step, 2, grad_values, lambda block: key_out.at[step, block, :, HD : 2 * HD])
+            sums[at] = summed
+        for extra in range(2):
+            sums[2 * half + extra] += part_in[step, EDGE_AT + 2 * half + extra].astype(jnp.float32)
+        for start in (EDGE_AT + 4, EDGE_AT + 6):
+            sums[3 * half] += part_in[step, start + half].astype(jnp.float32)
+        for at in range(HALF):
+            block = HALF * half + at
+            key_out[step, block] = sums[at].astype(jnp.bfloat16)
+            give(step, 1, grad_keys, key_out.at[step, block, :, 0:HD], block)
+            give(step, 2, grad_values, key_out.at[step, block, :, HD : 2 * HD], block)
 
     def find_bias():
         frame_blocks, listed = block_lists.shape[1], block_lists.shape[2]
@@ -357,8 +398,9 @@
         return carry
 
     lax.fori_loop(0, heads, stage, 0)
-    join_parts(heads - 1)
-    finish(heads - 1)
+    join_parts(heads - 1, 1 - backward)
+    finish(heads - 1, backward)
+    finish(heads - 1, 1 - backward)
 
     for at, result in enumerate((grad_queries, grad_keys, grad_values)):
         wait_for(result, out_recv.at[at])
@@ -397,9 +439,10 @@
                 pltpu.VMEM((heads, SLAB, 2 * BLK, 2 * HD), jnp.bfloat16),
                 pltpu.VMEM((heads, WINDOW, BLK, 2 * HD), jnp.bfloat16),
                 pltpu.VMEM((HD, WINDOW * BLK), jnp.bfloat16),
-                pltpu.VMEM((WINDOW, BLK, 2 * HD), jnp.float32),
+                pltpu.VMEM((OWN_WINDOW, BLK, 2 * HD), jnp.float32),
                 pltpu.VMEM((SLOTS * BLK, 2 * BLK), jnp.float32),
                 pltpu.VMEM((SLOTS * BLK, 2 * BLK), jnp.bfloat16),
+                pltpu.VMEM((HALF, BLK, 2 * HD), jnp.float32),
                 pltpu.SMEM((SLAB, SLOTS), jnp.float32),
                 pltpu.VMEM((heads, HALO_BLOCKS, BLK, 2 * HD), jnp.bfloat16),
                 pltpu.VMEM((heads, HALO_BLOCKS, BLK, 2 * HD), jnp.bfloat16),
@@ -410,7 +453,7 @@
                 pltpu.SemaphoreType.DMA((heads,)),
                 pltpu.SemaphoreType.DMA((heads, PEERS)),
                 pltpu.SemaphoreType.DMA((heads,)),
-                pltpu.SemaphoreType.DMA((heads, PEERS)),
+                pltpu.SemaphoreType.DMA((heads, PART_COPIES)),
                 pltpu.SemaphoreType.DMA((3,)),
                 pltpu.SemaphoreType.DMA((3,)),
             ],

time: 186 us -> 177 us (0.952); the launches traced: 185 us -> 174 us
  Pallas kernels: 178 us -> 167 us
    pallas_call x1, Pallas kernels: 178 us -> 167 us  [local(): pl.pallas_call(body, out_shape=(shape, shape, shape), in_specs=[pl.BlockS...]
where the time goes in v3:
time: 177 us; the launch traced here: 174 us
  Pallas kernels  167 us (94%)
  local copies, waits for them, and re-layouts  6.33 us (4%)
    pallas_call x1, Pallas kernels, local(): pl.pallas_call(body, out_shape=(shape, shape, shape), in_specs=[pl.BlockS...  167 us
    unnamed x8, local copies, waits for them, and re-layouts  6.33 us

profile of v3, /device:TPU:2, one launch (start us, length us, event | category | flops | bytes accessed | tf_op | source)
XLA Modules:
  0.0 173.6 jit_solution(14955397029566869709)
XLA Ops:
  0.6 1.4 copy.9.refs_0_
  2.0 166.6 %shard_map.85 = (bf16[128,4096]{1,0:T(8,128)(2,1)}, bf16[128,4096]{1,0:T(8,128)(2,1)}, bf16[128,4096]{1,0:T(8,128)(2,1)}) custom-call(s32[1,32,13]{2,1,0:T(8,128)} %copy.9.refs_0_, s32[1,32]{1,0:T(1,128)} %refs_1_.1, bf16[128,4096]{1,0:T(8,128)(2,1)} %refs_2_.1, bf16[128,4096]{1,0:T(8,128)(2,1)} %refs_3_.1, bf16[128,4096]{1,0:T(8,128)(2,1)} %refs_4_.1, ...), custom_call_target="tpu_custom_call" | custom-call | tf_op jit(solution)/shard_map/pallas_call | solution.py:433
  168.6 0.0 copy-start.1
  168.6 2.4 %copy.13 = bf16[128,4096]{1,0:T(8,128)(2,1)} copy(bf16[128,4096]{1,0:T(8,128)(2,1)} %get-tuple-element.6) | data formatting | bytes 2097152
  171.0 0.0 copy-done.1
  171.0 0.0 copy-start
  171.0 1.0 copy.14
  171.9 0.6 copy-done
  172.6 1.0 copy.15
Async XLA Ops:
  168.6 2.4 %copy-start.1 = (bf16[128,4096]{1,0:T(8,128)(2,1)S(1)}, bf16[128,4096]{1,0:T(8,128)(2,1)}, u32[]{:S(2)}) copy-start(bf16[128,4096]{1,0:T(8,128)(2,1)} %get-tuple-element.7) | copy-start | bytes 3145732
  171.0 1.6 copy-start

commit v4 on v3

--- a/solution.py
+++ b/solution.py
@@ -39,6 +39,7 @@
 JOIN = 32
 HALO_BLOCKS = 40
 PEERS = 4 + len(EDGES)
+PIECES = 4
 RING_ORDER = (4, 3, 5, 2, 6, 1, 7)
 
 
@@ -59,8 +60,8 @@
     frames,
     slabs,
     heads,
-    block_lists,
-    block_counts,
+    lists_in,
+    counts_in,
     queries,
     keys,
     values,
@@ -75,6 +76,8 @@
     raw,
     weights,
     sums,
+    block_lists,
+    block_counts,
     bias,
     part_out,
     part_in,
@@ -88,6 +91,7 @@
     part_recv,
     out_send,
     out_recv,
+    list_sem,
 ):
     frame = lax.axis_index("tm")
     space = lax.axis_index("space")
@@ -349,12 +353,12 @@
             give(step, 2, grad_values, key_out.at[step, block, :, HD : 2 * HD], block)
 
     def find_bias():
-        frame_blocks, listed = block_lists.shape[1], block_lists.shape[2]
+        listed, frame_blocks = block_lists.shape[0], block_lists.shape[2]
 
         def one(i, carry):
             block = slab * SLAB + i
             count = block_counts[0, block]
-            named = [jnp.where(at < count, block_lists[0, block, at], -1) for at in range(listed)]
+            named = [jnp.where(at < count, block_lists[at, 0, block], -1) for at in range(listed)]
             for slot in range(SLOTS):
                 to_frame, to_block = frame + FRAME_STEPS[slot], block + BLOCK_STEPS[slot]
                 wanted = to_frame * frame_blocks + to_block
@@ -375,6 +379,10 @@
     for frame_step, slab_step in steps + [entry[3:] for entry in EDGES]:
         device = neighbour(frame_step, slab_step)
         pl.semaphore_signal(barrier, inc=1, device_id=device, device_id_type=MESH)
+    fetch_lists = pltpu.make_async_copy(lists_in, block_lists, list_sem.at[0])
+    fetch_counts = pltpu.make_async_copy(counts_in, block_counts, list_sem.at[1])
+    fetch_lists.start()
+    fetch_counts.start()
     zeros = jnp.zeros((BLK, HD), jnp.bfloat16)
 
     def clear(at, carry):
@@ -383,11 +391,13 @@
         pairs[step, block, BLK : 2 * BLK, 0:HD] = zeros
         return carry
 
-    lax.fori_loop(0, heads * SLAB, clear, 0)
     pl.semaphore_wait(barrier, SLAB - 1 + PEERS)
 
     start_inputs(0)
     start_inputs(1)
+    lax.fori_loop(0, heads * SLAB, clear, 0)
+    fetch_lists.wait()
+    fetch_counts.wait()
     find_bias()
     start_halo(0)
     start_inputs(2)
@@ -417,12 +427,32 @@
     lax.fori_loop(0, heads, drain, 0)
 
 
+def hand_over(*refs):
+    sources, targets, (held, in_sem, out_sem) = refs[:3], refs[3:6], refs[6:]
+    rows = held.shape[1] // PIECES
+    pieces = [(at, piece, slice(piece * rows, (piece + 1) * rows)) for at in range(3) for piece in range(PIECES)]
+    arriving = [
+        pltpu.make_async_copy(sources[at].at[span], held.at[at, span], in_sem.at[at, piece]) for at, piece, span in pieces
+    ]
+    leaving = [
+        pltpu.make_async_copy(held.at[at, span], targets[at].at[span], out_sem.at[at, piece]) for at, piece, span in pieces
+    ]
+    for copy in arriving:
+        copy.start()
+    for copy, then in zip(arriving, leaving):
+        copy.wait()
+        then.start()
+    for copy in leaving:
+        copy.wait()
+
+
 def solution(mesh):
     frames = mesh.shape["tm"]
     slabs = mesh.shape["space"] // SLAB
 
     def local(queries, key_rows, value_rows, grads_out, block_lists, block_counts):
         rows, width = queries.shape
+        block_lists = jnp.transpose(block_lists, (2, 0, 1))
         heads = width // HD // SLAB
         shape = jax.ShapeDtypeStruct((rows, width), jnp.bfloat16)
         anywhere = pl.BlockSpec(memory_space=pl.ANY)
@@ -430,10 +460,10 @@
         def body(*refs):
             kernel(frames, slabs, heads, *refs)
 
-        return pl.pallas_call(
+        grads = pl.pallas_call(
             body,
             out_shape=(shape, shape, shape),
-            in_specs=[pl.BlockSpec(memory_space=pltpu.SMEM)] * 2 + [anywhere] * 4,
+            in_specs=[anywhere] * 6,
             out_specs=(anywhere, anywhere, anywhere),
             scratch_shapes=[
                 pltpu.VMEM((heads, SLAB, 2 * BLK, 2 * HD), jnp.bfloat16),
@@ -443,6 +473,8 @@
                 pltpu.VMEM((SLOTS * BLK, 2 * BLK), jnp.float32),
                 pltpu.VMEM((SLOTS * BLK, 2 * BLK), jnp.bfloat16),
                 pltpu.VMEM((HALF, BLK, 2 * HD), jnp.float32),
+                pltpu.SMEM(block_lists.shape, jnp.int32),
+                pltpu.SMEM(block_counts.shape, jnp.int32),
                 pltpu.SMEM((SLAB, SLOTS), jnp.float32),
                 pltpu.VMEM((heads, HALO_BLOCKS, BLK, 2 * HD), jnp.bfloat16),
                 pltpu.VMEM((heads, HALO_BLOCKS, BLK, 2 * HD), jnp.bfloat16),
@@ -456,11 +488,24 @@
                 pltpu.SemaphoreType.DMA((heads, PART_COPIES)),
                 pltpu.SemaphoreType.DMA((3,)),
                 pltpu.SemaphoreType.DMA((3,)),
+                pltpu.SemaphoreType.DMA((2,)),
             ],
             compiler_params=pltpu.CompilerParams(
                 collective_id=0, has_side_effects=True, vmem_limit_bytes=60 * 1024 * 1024
             ),
         )(block_lists, block_counts, queries, key_rows, value_rows, grads_out)
+        return pl.pallas_call(
+            hand_over,
+            out_shape=(shape, shape, shape),
+            in_specs=[anywhere] * 3,
+            out_specs=(anywhere, anywhere, anywhere),
+            scratch_shapes=[
+                pltpu.VMEM((3, rows, width), jnp.bfloat16),
+                pltpu.SemaphoreType.DMA((3, PIECES)),
+                pltpu.SemaphoreType.DMA((3, PIECES)),
+            ],
+            compiler_params=pltpu.CompilerParams(vmem_limit_bytes=60 * 1024 * 1024),
+        )(*grads)
 
     rows = P(("tm", "space"), None)
     return jax.shard_map(

time: 177 us -> 173 us (0.977)
  local copies, waits for them, and re-layouts: 6.33 us -> 0 us
  Pallas kernels: 167 us -> 169 us
    unnamed x8 -> x0, local copies, waits for them, and re-layouts: 6.33 us -> none
    pallas_call x1 -> x2, Pallas kernels: 167 us -> 169 us  [the longest x1 166 us: local(): pl.pallas_call(body, out_shape=(shape, shape, shape), in_specs=[anywhere]...]
where the time goes in v4:
time: 173 us; the launch traced here: 169 us
  Pallas kernels  169 us (98%)
    pallas_call x1, Pallas kernels, local(): pl.pallas_call(body, out_shape=(shape, shape, shape), in_specs=[anywhere]...  166 us

profile of v4, /device:TPU:2, one launch (start us, length us, event | category | flops | bytes accessed | tf_op | source)
XLA Modules:
  0.0 169.2 jit_solution(10775392985408445725)
XLA Ops:
  0.6 165.8 %shard_map.85 = (bf16[128,4096]{1,0:T(8,128)(2,1)}, bf16[128,4096]{1,0:T(8,128)(2,1)}, bf16[128,4096]{1,0:T(8,128)(2,1)}) custom-call(s32[13,1,32]{2,1,0:T(1,128)} %bitcast.1, s32[1,32]{1,0:T(1,128)} %refs_1_.1, bf16[128,4096]{1,0:T(8,128)(2,1)} %refs_2_.1, bf16[128,4096]{1,0:T(8,128)(2,1)} %refs_3_.1, bf16[128,4096]{1,0:T(8,128)(2,1)} %refs_4_.1, ...), custom_call_target="tpu_custom_call" | custom-call | tf_op jit(solution)/shard_map/pallas_call | solution.py:463
  166.4 2.8 %shard_map.86 = (bf16[128,4096]{1,0:T(8,128)(2,1)}, bf16[128,4096]{1,0:T(8,128)(2,1)}, bf16[128,4096]{1,0:T(8,128)(2,1)}) custom-call(bf16[128,4096]{1,0:T(8,128)(2,1)} %get-tuple-element.6.refs_0_, bf16[128,4096]{1,0:T(8,128)(2,1)} %get-tuple-element.7.refs_1_, bf16[128,4096]{1,0:T(8,128)(2,1)} %get-tuple-element.8.refs_2_), custom_call_target="tpu_custom_call" | custom-call | tf_op jit(solution)/shard_map/pallas_call | solution.py:497

commit v5 on v4

--- a/solution.py
+++ b/solution.py
@@ -39,7 +39,6 @@
 JOIN = 32
 HALO_BLOCKS = 40
 PEERS = 4 + len(EDGES)
-PIECES = 4
 RING_ORDER = (4, 3, 5, 2, 6, 1, 7)
 
 
@@ -250,11 +249,11 @@
                     part_out[step, start + i, :, 0:HD] = (update[:, 0:HD] * SCALE).astype(jnp.bfloat16)
                     part_out[step, start + i, :, HD : 2 * HD] = update[:, HD : 2 * HD].astype(jnp.bfloat16)
             query_out[step, i] = (grad_query * SCALE).T.astype(jnp.bfloat16)
-            give(step, 0, grad_queries, query_out.at[step, i], i)
 
             @pl.when(turn == HALF - 1)
             def _():
                 send_far(step, backward)
+                give_queries(step, backward)
 
             @pl.when(turn == HALF + 1)
             def _():
@@ -267,6 +266,7 @@
 
         send_far(step, 1 - backward)
         send_near(step, 1 - backward, backward)
+        give_queries(step, 1 - backward)
 
     def send_part(step, start, count, at, device):
         send(
@@ -329,6 +329,11 @@
         @pl.when(there != place)
         def _():
             send(tile, target, out_send.at[at], out_recv.at[at], (frame, slab * SLAB + there))
+
+    def give_queries(step, half):
+        for at in range(HALF):
+            block = HALF * half + lax.rem(place + at, HALF)
+            give(step, 0, grad_queries, query_out.at[step, block], block)
 
     def finish(step, half):
         for at, start in ((INNER, 0), (OUTER, SLAB), (OUTER2, 2 * SLAB)):
@@ -347,8 +352,9 @@
         for start in (EDGE_AT + 4, EDGE_AT + 6):
             sums[3 * half] += part_in[step, start + half].astype(jnp.float32)
         for at in range(HALF):
-            block = HALF * half + at
-            key_out[step, block] = sums[at].astype(jnp.bfloat16)
+            key_out[step, HALF * half + at] = sums[at].astype(jnp.bfloat16)
+        for at in range(HALF):
+            block = HALF * half + lax.rem(place + at, HALF)
             give(step, 1, grad_keys, key_out.at[step, block, :, 0:HD], block)
             give(step, 2, grad_values, key_out.at[step, block, :, HD : 2 * HD], block)
 
@@ -428,21 +434,11 @@
 
 
 def hand_over(*refs):
-    sources, targets, (held, in_sem, out_sem) = refs[:3], refs[3:6], refs[6:]
-    rows = held.shape[1] // PIECES
-    pieces = [(at, piece, slice(piece * rows, (piece + 1) * rows)) for at in range(3) for piece in range(PIECES)]
-    arriving = [
-        pltpu.make_async_copy(sources[at].at[span], held.at[at, span], in_sem.at[at, piece]) for at, piece, span in pieces
-    ]
-    leaving = [
-        pltpu.make_async_copy(held.at[at, span], targets[at].at[span], out_sem.at[at, piece]) for at, piece, span in pieces
-    ]
-    for copy in arriving:
+    sources, targets, sem = refs[:3], refs[3:6], refs[6]
+    copies = [pltpu.make_async_copy(sources[at], targets[at], sem.at[at]) for at in range(3)]
+    for copy in copies:
         copy.start()
-    for copy, then in zip(arriving, leaving):
-        copy.wait()
-        then.start()
-    for copy in leaving:
+    for copy in copies:
         copy.wait()
 
 
@@ -456,15 +452,16 @@
         heads = width // HD // SLAB
         shape = jax.ShapeDtypeStruct((rows, width), jnp.bfloat16)
         anywhere = pl.BlockSpec(memory_space=pl.ANY)
+        vmem = pl.BlockSpec(memory_space=pltpu.VMEM)
 
         def body(*refs):
             kernel(frames, slabs, heads, *refs)
 
         grads = pl.pallas_call(
             body,
-            out_shape=(shape, shape, shape),
+            out_shape=(pltpu.VMEM((rows, width), jnp.bfloat16),) * 3,
             in_specs=[anywhere] * 6,
-            out_specs=(anywhere, anywhere, anywhere),
+            out_specs=(vmem, vmem, vmem),
             scratch_shapes=[
                 pltpu.VMEM((heads, SLAB, 2 * BLK, 2 * HD), jnp.bfloat16),
                 pltpu.VMEM((heads, WINDOW, BLK, 2 * HD), jnp.bfloat16),
@@ -497,15 +494,11 @@
         return pl.pallas_call(
             hand_over,
             out_shape=(shape, shape, shape),
-            in_specs=[anywhere] * 3,
+            in_specs=[vmem] * 3,
             out_specs=(anywhere, anywhere, anywhere),
-            scratch_shapes=[
-                pltpu.VMEM((3, rows, width), jnp.bfloat16),
-                pltpu.SemaphoreType.DMA((3, PIECES)),
-                pltpu.SemaphoreType.DMA((3, PIECES)),
-            ],
-            compiler_params=pltpu.CompilerParams(vmem_limit_bytes=60 * 1024 * 1024),
-        )(*grads)
+            scratch_shapes=[pltpu.SemaphoreType.DMA((3,))],
+            compiler_params=pltpu.CompilerParams(vmem_limit_bytes=32 * 1024 * 1024),
+        )(*[pltpu.with_memory_space_constraint(grad, pltpu.VMEM) for grad in grads])
 
     rows = P(("tm", "space"), None)
     return jax.shard_map(

time: 173 us -> 171 us (0.988)
  no operation moved by 1% of the time
where the time goes in v5:
time: 171 us; the launch traced here: 168 us
  Pallas kernels  168 us (98%)
    pallas_call x1, Pallas kernels, local(): pl.pallas_call(body, out_shape=(pltpu.VMEM((rows, width), jnp.bfloat16),)...  166 us

profile of v5, /device:TPU:2, one launch (start us, length us, event | category | flops | bytes accessed | tf_op | source)
XLA Modules:
  0.0 168.5 jit_solution(16285776155259608000)
XLA Ops:
  0.6 166.2 %shard_map.85 = (bf16[128,4096]{1,0:T(8,128)(2,1)S(1)}, bf16[128,4096]{1,0:T(8,128)(2,1)S(1)}, bf16[128,4096]{1,0:T(8,128)(2,1)S(1)}) custom-call(s32[13,1,32]{2,1,0:T(1,128)} %bitcast.1, s32[1,32]{1,0:T(1,128)} %refs_1_.1, bf16[128,4096]{1,0:T(8,128)(2,1)} %refs_2_.1, bf16[128,4096]{1,0:T(8,128)(2,1)} %refs_3_.1, bf16[128,4096]{1,0:T(8,128)(2,1)} %refs_4_.1, ...), custom_call_target="tpu_custom_call" | custom-call | tf_op jit(solution)/shard_map/pallas_call | solution.py:460
  166.8 1.7 %shard_map.86 = (bf16[128,4096]{1,0:T(8,128)(2,1)}, bf16[128,4096]{1,0:T(8,128)(2,1)}, bf16[128,4096]{1,0:T(8,128)(2,1)}) custom-call(bf16[128,4096]{1,0:T(8,128)(2,1)S(1)} %get-tuple-element.6.refs_0_, bf16[128,4096]{1,0:T(8,128)(2,1)S(1)} %get-tuple-element.7.refs_1_, bf16[128,4096]{1,0:T(8,128)(2,1)S(1)} %get-tuple-element.8.refs_2_), custom_call_target="tpu_custom_call" | custom-call | tf_op jit(solution)/shard_map/pallas_call | solution.py:494

commit v6 on v5

--- a/solution.py
+++ b/solution.py
@@ -193,10 +193,6 @@
             def _():
                 start_halo(step + 1)
 
-            @pl.when((turn == 2) & (step + 3 < heads))
-            def _():
-                start_inputs(step + 3)
-
             @pl.when((turn == 3) & (step >= 1))
             def _():
                 finish(step - 1, backward)
@@ -253,7 +249,6 @@
             @pl.when(turn == HALF - 1)
             def _():
                 send_far(step, backward)
-                give_queries(step, backward)
 
             @pl.when(turn == HALF + 1)
             def _():
@@ -266,7 +261,7 @@
 
         send_far(step, 1 - backward)
         send_near(step, 1 - backward, backward)
-        give_queries(step, 1 - backward)
+        give_queries(step)
 
     def send_part(step, start, count, at, device):
         send(
@@ -330,10 +325,10 @@
         def _():
             send(tile, target, out_send.at[at], out_recv.at[at], (frame, slab * SLAB + there))
 
-    def give_queries(step, half):
-        for at in range(HALF):
-            block = HALF * half + lax.rem(place + at, HALF)
-            give(step, 0, grad_queries, query_out.at[step, block], block)
+    def give_queries(step):
+        for distance in RING_ORDER + (0,):
+            there = lax.rem(place + distance, SLAB)
+            give(step, 0, grad_queries, query_out.at[step, there], there)
 
     def finish(step, half):
         for at, start in ((INNER, 0), (OUTER, SLAB), (OUTER2, 2 * SLAB)):
@@ -401,12 +396,13 @@
 
     start_inputs(0)
     start_inputs(1)
+    start_inputs(2)
+    start_inputs(3)
     lax.fori_loop(0, heads * SLAB, clear, 0)
     fetch_lists.wait()
     fetch_counts.wait()
     find_bias()
     start_halo(0)
-    start_inputs(2)
     pass_halo(0)
 
     def stage(step, carry):
@@ -417,20 +413,20 @@
     join_parts(heads - 1, 1 - backward)
     finish(heads - 1, backward)
     finish(heads - 1, 1 - backward)
+
+    def drain(step, carry):
+        wait_for(window.at[step, 0 : (SLAB - 1) * 2], in_send.at[step])
+        wait_for(window.at[step, 0:HALO_BLOCKS], halo_send.at[step])
+        wait_for(part_in.at[step], part_send.at[step])
+        return carry
+
+    lax.fori_loop(0, heads, drain, 0)
 
     for at, result in enumerate((grad_queries, grad_keys, grad_values)):
         wait_for(result, out_recv.at[at])
     sent_tiles = (SLAB - 1) * heads // 2
     for at in range(3):
         wait_for(window.at[0, 0:sent_tiles], out_send.at[at])
-
-    def drain(step, carry):
-        wait_for(window.at[step, 0 : (SLAB - 1) * 2], in_send.at[step])
-        wait_for(window.at[step, 0:HALO_BLOCKS], halo_send.at[step])
-        wait_for(part_in.at[step], part_send.at[step])
-        return carry
-
-    lax.fori_loop(0, heads, drain, 0)
 
 
 def hand_over(*refs):

time: 171 us -> 171 us (level)
  no operation moved by 1% of the time
where the time goes in v6:
time: 171 us; the launch traced here: 168 us
  Pallas kernels  168 us (98%)
    pallas_call x1, Pallas kernels, local(): pl.pallas_call(body, out_shape=(pltpu.VMEM((rows, width), jnp.bfloat16),)...  166 us

profile of v6, /device:TPU:2, one launch (start us, length us, event | category | flops | bytes accessed | tf_op | source)
XLA Modules:
  0.0 168.4 jit_solution(13696855257528533103)
XLA Ops:
  0.6 166.1 %shard_map.85 = (bf16[128,4096]{1,0:T(8,128)(2,1)S(1)}, bf16[128,4096]{1,0:T(8,128)(2,1)S(1)}, bf16[128,4096]{1,0:T(8,128)(2,1)S(1)}) custom-call(s32[13,1,32]{2,1,0:T(1,128)} %bitcast.1, s32[1,32]{1,0:T(1,128)} %refs_1_.1, bf16[128,4096]{1,0:T(8,128)(2,1)} %refs_2_.1, bf16[128,4096]{1,0:T(8,128)(2,1)} %refs_3_.1, bf16[128,4096]{1,0:T(8,128)(2,1)} %refs_4_.1, ...), custom_call_target="tpu_custom_call" | custom-call | tf_op jit(solution)/shard_map/pallas_call | solution.py:456
  166.8 1.7 %shard_map.86 = (bf16[128,4096]{1,0:T(8,128)(2,1)}, bf16[128,4096]{1,0:T(8,128)(2,1)}, bf16[128,4096]{1,0:T(8,128)(2,1)}) custom-call(bf16[128,4096]{1,0:T(8,128)(2,1)S(1)} %get-tuple-element.6.refs_0_, bf16[128,4096]{1,0:T(8,128)(2,1)S(1)} %get-tuple-element.7.refs_1_, bf16[128,4096]{1,0:T(8,128)(2,1)S(1)} %get-tuple-element.8.refs_2_), custom_call_target="tpu_custom_call" | custom-call | tf_op jit(solution)/shard_map/pallas_call | solution.py:490

commit v7 on v5

--- a/solution.py
+++ b/solution.py
@@ -131,11 +131,12 @@
             window.at[step, 2 + place, :, 0:HD],
             window.at[step, 2 + place, :, HD : 2 * HD],
         )
-        for distance in RING_ORDER:
-            there, device = ring(distance)
-            for at, source in ((2, keys), (3, values), (0, queries), (1, grads)):
+        for group in (((2, keys), (3, values)), ((0, queries), (1, grads))):
+            for distance in RING_ORDER:
+                there, device = ring(distance)
                 columns = head_columns(there, step)
-                send(source.at[:, columns], landing[at], in_send.at[step], in_recv.at[step, at], device)
+                for at, source in group:
+                    send(source.at[:, columns], landing[at], in_send.at[step], in_recv.at[step, at], device)
         for at, source in enumerate((queries, grads, keys, values)):
             columns = head_columns(place, step)
             pltpu.make_async_copy(source.at[:, columns], landing[at], in_recv.at[step, at]).start()

time: 171 us -> 171 us (level)
  no operation moved by 1% of the time
where the time goes in v7:
time: 171 us; the launch traced here: 168 us
  Pallas kernels  168 us (98%)
    pallas_call x1, Pallas kernels, local(): pl.pallas_call(body, out_shape=(pltpu.VMEM((rows, width), jnp.bfloat16),)...  166 us

profile of v7, /device:TPU:2, one launch (start us, length us, event | category | flops | bytes accessed | tf_op | source)
XLA Modules:
  0.0 168.5 jit_solution(7365559987062157388)
XLA Ops:
  0.6 166.1 %shard_map.85 = (bf16[128,4096]{1,0:T(8,128)(2,1)S(1)}, bf16[128,4096]{1,0:T(8,128)(2,1)S(1)}, bf16[128,4096]{1,0:T(8,128)(2,1)S(1)}) custom-call(s32[13,1,32]{2,1,0:T(1,128)} %bitcast.1, s32[1,32]{1,0:T(1,128)} %refs_1_.1, bf16[128,4096]{1,0:T(8,128)(2,1)} %refs_2_.1, bf16[128,4096]{1,0:T(8,128)(2,1)} %refs_3_.1, bf16[128,4096]{1,0:T(8,128)(2,1)} %refs_4_.1, ...), custom_call_target="tpu_custom_call" | custom-call | tf_op jit(solution)/shard_map/pallas_call | solution.py:461
  166.8 1.7 %shard_map.86 = (bf16[128,4096]{1,0:T(8,128)(2,1)}, bf16[128,4096]{1,0:T(8,128)(2,1)}, bf16[128,4096]{1,0:T(8,128)(2,1)}) custom-call(bf16[128,4096]{1,0:T(8,128)(2,1)S(1)} %get-tuple-element.6.refs_0_, bf16[128,4096]{1,0:T(8,128)(2,1)S(1)} %get-tuple-element.7.refs_1_, bf16[128,4096]{1,0:T(8,128)(2,1)S(1)} %get-tuple-element.8.refs_2_), custom_call_target="tpu_custom_call" | custom-call | tf_op jit(solution)/shard_map/pallas_call | solution.py:495
